TPU v7x, 32 devices: a whole 2x2x4 slice. The times are simulated.
32 devices in a mesh: section: 2 (over core), dp: 4 (over z), tensor: 4 (over y, x).
Axes of the slice: x: 2, y: 2, z: 4, core: 2. Of those that a mesh axis runs over, the one named last changes fastest.
Arguments:
- inputs: bfloat16 [96, 160, 768], P(('dp', 'tensor')), may hold values from -6 to 6
- lengths: int32 [96], P('dp'), may hold values from 95 to 160, as said below
- cotangent: bfloat16 [96, 160, 768], P(('dp', 'tensor')), may hold values from -6 to 6
- w_qkv: bfloat16 [2, 3, 768, 768], P('section', None, None, 'tensor'), may hold values from -0.21875 to 0.21875
- qv_bias: float32 [2, 2, 12, 64], P('section', None, 'tensor'), may hold values from -3 to 3
- w_out: bfloat16 [2, 768, 768], P('section', 'tensor'), may hold values from -1.25 to 1.25
- out_bias: float32 [2, 768], P('section'), may hold values from -2 to 2
- ln1_gain: float32 [2, 768], P('section'), may hold values from 0.25 to 1.75
- ln1_bias: float32 [2, 768], P('section'), may hold values from -2 to 2
- w_up: bfloat16 [2, 768, 3072], P('section', None, 'tensor'), may hold values from -0.21875 to 0.21875
- up_bias: float32 [2, 48, 64], P('section', 'tensor'), may hold values from -3 to 3
- w_down: bfloat16 [2, 3072, 768], P('section', 'tensor'), may hold values from -0.15625 to 0.15625
- down_bias: float32 [2, 768], P('section'), may hold values from -2 to 2
- ln2_gain: float32 [2, 768], P('section'), may hold values from 0.25 to 1.75
- ln2_bias: float32 [2, 768], P('section'), may hold values from -2 to 2
Outputs:
- layer_outputs: bfloat16 [2, 96, 160, 768], P('section', ('dp', 'tensor'))
- input_grads: bfloat16 [2, 96, 160, 768], P('section', ('dp', 'tensor'))
- grad_qkv: float32 [2, 3, 768, 768], P('section', None, 'dp', 'tensor')
- grad_qv_bias: float32 [2, 2, 12, 64], P('section', None, 'tensor', 'dp')
- grad_out: float32 [2, 768, 768], P('section', 'tensor', 'dp')
- grad_up: float32 [2, 768, 3072], P('section', 'dp', 'tensor')
- grad_up_bias: float32 [2, 48, 64], P('section', 'tensor', 'dp')
- grad_down: float32 [2, 3072, 768], P('section', 'tensor', 'dp')
- grad_vectors: float32 [2, 6, 768], P('section', None, ('dp', 'tensor'))
- chain_rms: float32 [2, 3, 96], P('section', None, ('dp', 'tensor'))
Inputs may be any that keep to these rules, and one draw needn't show every extreme that they name: `lengths`: among the 24 chains of one index of dp, one chain has exactly 160 valid residues and another exactly 95.
All inputs are finite; a program needn't handle non-finite values.
Results may differ from a plain program's by a relative error of at most 0.025.
Values may be sent and summed in bfloat16 or wider, within the bound.
A program may use at most 192 MiB of HBM per device.

v0:
```python
import functools

import jax
import jax.numpy as jnp
from jax import lax
from jax.experimental import pallas as pl
from jax.experimental.pallas import tpu as pltpu
from jax.sharding import PartitionSpec as P


f32, bf16 = jnp.float32, jnp.bfloat16
D, FB, HB, HS = 768, 768, 192, 64
NT = (((1,), (1,)), ((), ()))
NN = (((1,), (0,)), ((), ()))
TN = (((0,), (0,)), ((), ()))
EPS_NORM, EPS_ROOT = 1e-12, 1e-6
MASK_FILL = -1e9
ROOT_HALF, INV_ROOT_TWO_PI = 0.7071067811865476, 0.3989422804014327
MESH = pl.DeviceIdType.MESH
KA, KU, KD = 0, 1, 2
HPB = HB // HS


def dot(a, b, dims=NN):
    return lax.dot_general(a, b, dims, preferred_element_type=f32)


def rows(i, n):
    return pl.ds(pl.multiple_of(i * n, n), n)


def mean_last(v):
    return jnp.mean(v, axis=-1, keepdims=True)


def rms_rows(v):
    return jnp.sqrt(mean_last(v * v) + EPS_ROOT)


def norm_step(x, gain, bias):
    c = x - mean_last(x)
    inv = lax.rsqrt(mean_last(c * c) + EPS_NORM)
    u = c * inv
    return u * gain + bias, u, inv


def norm_back(dn, u, inv, gain):
    du = dn * gain
    return inv * (du - mean_last(du) - u * mean_last(du * u))


def part8(v):
    t = v[0:8]
    for i in range(1, v.shape[0] // 8):
        t = t + v[8 * i:8 * (i + 1)]
    return t


def col_sum(v):
    return jnp.sum(part8(v), axis=0, keepdims=True)


def row_block(M):
    for n in (96, 80, 64, 48, 32, 16):
        if M % n == 0:
            return n
    return M


def attn_fwd_block(x_ref, wa_ref, sp_ref, kb_ref, qkv_ref, a_ref, c_ref, acc_ref, nch, L):
    qkv_ref[...] = (dot(x_ref[...], wa_ref[0:3 * HB, :], NT) + sp_ref[1:2, 0:3 * HB]).astype(bf16)
    for c in range(nch):
        rs = slice(c * L, (c + 1) * L)
        qkv = qkv_ref[rs, :]
        kb = kb_ref[c:c + 1, :]

        def head(t, i):
            return qkv[:, t * HB + i * HS:t * HB + (i + 1) * HS]
        scores = [dot(head(0, i), head(1, i), NT) * (HS ** -0.5) + kb for i in range(HPB)]
        probs = []
        for i in range(HPB):
            e = jnp.exp(scores[i] - jnp.max(scores[i], axis=-1, keepdims=True))
            a = (e / jnp.sum(e, axis=-1, keepdims=True)).astype(bf16)
            a_ref[c, i] = a
            probs.append(a)
        c_ref[rs, :] = jnp.concatenate([dot(probs[i], head(2, i)).astype(bf16) for i in range(HPB)], axis=1)
    acc_ref[...] += dot(c_ref[...], wa_ref[3 * HB:4 * HB, :])


def ln1_fwd(x_ref, acc_ref, sp_ref, u_ref, inv_ref, nlow_ref, rms_ref, M):
    rb = M // 3 if M % 48 == 0 else M

    def body(i, _):
        rs = rows(i, rb)
        h = x_ref[rs, :].astype(f32)
        att = acc_ref[rs, :] + sp_ref[2:3, :]
        n, u, inv = norm_step(h + att, sp_ref[3:4, :], sp_ref[4:5, :])
        u_ref[rs, :] = u
        inv_ref[rs, :] = inv
        nlow_ref[rs, :] = n.astype(bf16)
        rms_ref[0, rs, :] = rms_rows(h)
        rms_ref[1, rs, :] = rms_rows(att)
        return 0
    lax.fori_loop(0, M // rb, body, 0)


def up_block(nlow_ref, wu_ref, sp_ref, g_ref, gp_ref):
    for j in range(FB // 256):
        js = slice(256 * j, 256 * (j + 1))
        z = dot(nlow_ref[...], wu_ref[:, js]) + sp_ref[0:1, js]
        cdf = 0.5 * (1.0 + lax.erf(z * ROOT_HALF))
        g_ref[:, js] = (z * cdf).astype(bf16)
        gp_ref[:, js] = cdf + z * (INV_ROOT_TWO_PI * jnp.exp(-0.5 * z * z))


def down_block(g_ref, wd_ref, acc_ref):
    acc_ref[...] += dot(g_ref[...], wd_ref[...])


def ln2_fwd(u1_ref, acc_ref, sp_ref, u_ref, inv_ref, y_ref, rms_ref, M):
    rb = M // 3 if M % 48 == 0 else M

    def body(i, _):
        rs = rows(i, rb)
        n = u1_ref[rs, :] * sp_ref[3:4, :] + sp_ref[4:5, :]
        ffn = acc_ref[rs, :] + sp_ref[5:6, :]
        y, u, inv = norm_step(n + ffn, sp_ref[6:7, :], sp_ref[7:8, :])
        u_ref[rs, :] = u
        inv_ref[rs, :] = inv
        y_ref[rs, :] = y.astype(bf16)
        rms_ref[2, rs, :] = rms_rows(ffn)
        return 0
    lax.fori_loop(0, M // rb, body, 0)


def norm_bwd(dy_ref, u_ref, inv_ref, gain, dx_ref, low_ref, sm_ref, row, M):
    rb = row_block(M)

    def body(i, carry):
        a, b, c = carry
        rs = rows(i, rb)
        dy = dy_ref[rs, :].astype(f32)
        u = u_ref[rs, :]
        dx = norm_back(dy, u, inv_ref[rs, :], gain)
        dx_ref[rs, :] = dx
        low_ref[rs, :] = dx.astype(bf16)
        return (a + part8(dx), b + part8(dy * u), c + part8(dy))
    z = jnp.zeros((8, D), f32)
    sums = lax.fori_loop(0, M // rb, body, (z, z, z))
    for k in range(3):
        sm_ref[row + k:row + k + 1, :] = jnp.sum(sums[k], axis=0, keepdims=True)


def ffn_bwd_block(df_ref, wu_ref, wd_ref, gp_ref, dz_ref, dx_ref, ub_ref):
    for j in range(FB // 256):
        js = slice(256 * j, 256 * (j + 1))
        dz = (dot(df_ref[...], wd_ref[js, :], NT) * gp_ref[:, js]).astype(bf16)
        dz_ref[:, js] = dz
        ub_ref[:, js] = col_sum(dz.astype(f32))
    dx_ref[...] += dot(dz_ref[...], wu_ref[...], NT)


def attn_bwd_block(da_ref, wa_ref, qkv_ref, a_ref, dc_ref, dqkv_ref, dx_ref, qb_ref, nch, L):
    dc_ref[...] = dot(da_ref[...], wa_ref[3 * HB:4 * HB, :], NT).astype(bf16)
    for c in range(nch):
        rs = slice(c * L, (c + 1) * L)
        qkv = qkv_ref[rs, :]
        dc = dc_ref[rs, :]

        def head(t, i):
            return qkv[:, t * HB + i * HS:t * HB + (i + 1) * HS]
        dcs = [dc[:, i * HS:(i + 1) * HS] for i in range(HPB)]
        probs = [a_ref[c, i] for i in range(HPB)]
        drs = [dot(dcs[i], head(2, i), NT) for i in range(HPB)]
        dss = []
        for i in range(HPB):
            af = probs[i].astype(f32)
            t = af * drs[i]
            dss.append(((t - af * jnp.sum(t, axis=-1, keepdims=True)) * (HS ** -0.5)).astype(bf16))
        dqs = [dot(dss[i], head(1, i)) for i in range(HPB)]
        dks = [dot(dss[i], head(0, i), TN) for i in range(HPB)]
        dvs = [dot(probs[i], dcs[i], TN) for i in range(HPB)]
        dqkv_ref[rs, :] = jnp.concatenate(dqs + dks + dvs, axis=1).astype(bf16)
    dx_ref[...] += dot(dqkv_ref[...], wa_ref[0:3 * HB, :])
    qb_ref[:, 0:3 * HB] = col_sum(dqkv_ref[...].astype(f32))
ZR = 224
XY = D - ZR


def k1_kernel(nch, L,
              len_ref, x_in, wq_in, wo_in, wu_in, wd_in, qv_in, ub_in, v0_in, v1_in, v2_in, v3_in, v4_in, v5_in,
              w_out, sp_out, qkv_out, a_out, c_out, u_out, inv_out, g_out, gp_out, y_out, rms_out,
              wv, spv, xb, qkv, a, c, u, inv, g, gp, nlow, acc, rms, rmsv, wa_in, sp_in, qv, ub, vecs, kb_ref,
              recv, send, sp_recv, sp_send, loc, wsave, ssave, pre, go):
    M = nch * L
    s = lax.axis_index("section")
    t = lax.axis_index("tensor")
    xn = {"tensor": t + 1 - 2 * lax.rem(t, 2)}
    yn = {"tensor": t + 2 - 4 * lax.rem(t // 2, 2)}
    j = lax.axis_index("dp")
    sib = {"section": 1 - s}
    zn = {"dp": j + 1 - 2 * lax.rem(j, 2)}
    diag = {"tensor": 3 - t}
    e = lax.rem(j, 2)
    srcs = (wa_in, wu_in, wd_in)

    def remote(src, dst, ss, rs, dev):
        return pltpu.make_async_remote_copy(src_ref=src, dst_ref=dst, send_sem=ss, recv_sem=rs, device_id=dev, device_id_type=MESH)

    def span(start, n):
        return pl.ds(pl.multiple_of(start, 16), n)
    fetched = span(e * ZR, XY)
    half = [span(e * ZR + i * (XY // 2), XY // 2) for i in range(2)]
    given = span(e * XY, ZR)
    taken = span((1 - e) * XY, ZR)

    def view(ref, p):
        if p == 0:
            return ref.at[0]
        if p in (1, 2):
            return ref.at[p, fetched]
        if p in (3, 4):
            return ref.at[3, half[p - 3]]
        return ref.at[p - 4, taken]

    def part(l, k, p):
        return view(wv.at[l, k], p)

    def wait_part(l, k, p):
        ref = part(l, k, p)
        pltpu.make_async_copy(ref, ref, recv.at[l, k, p]).wait()

    def own_sends(l, k):
        return [remote(srcs[k].at[fetched], wv.at[l, k, 1, fetched], send.at[k, 0], recv.at[l, k, 1], xn),
                remote(srcs[k].at[fetched], wv.at[l, k, 2, fetched], send.at[k, 1], recv.at[l, k, 2], yn)]

    def own_local(l, k):
        return remote(srcs[k], wv.at[l, k, 0], send.at[k, 7], recv.at[l, k, 0], sib)

    def fwd_y(l, k):
        return remote(wv.at[l, k, 1, half[0]], wv.at[l, k, 3, half[0]], send.at[k, 2], recv.at[l, k, 3], yn)

    def fwd_x(l, k):
        return remote(wv.at[l, k, 2, half[1]], wv.at[l, k, 3, half[1]], send.at[k, 3], recv.at[l, k, 4], xn)

    def to_z(l, k, slot):
        ref = wv.at[l, k, slot, given]
        return remote(ref, ref, send.at[k, 3 + slot], recv.at[l, k, 4 + slot], zn)

    def to_sib(l, k, p):
        return remote(part(l, k, p), part(l, k, p), send.at[k, 7 + p], recv.at[l, k, p], sib)

    def save_w(l, k, p):
        return pltpu.make_async_copy(part(l, k, p), view(w_out.at[l, k], p), wsave.at[l, k, p])

    def arrive(l, k, p):
        wait_part(l, k, p)

        @pl.when(s == l)
        def _():
            if p == 1:
                fwd_y(l, k).start()
                to_z(l, k, 1).start()
            if p == 2:
                fwd_x(l, k).start()
                to_z(l, k, 2).start()
                if k == KA:
                    for d in own_sends(l, KD):
                        d.start()
            if p in (3, 4):
                @pl.when(e == p - 3)
                def _():
                    to_z(l, k, 3).start()
            if p > 0:
                to_sib(l, k, p).start()
        save_w(l, k, p).start()

    others = [(q, {"section": sec, "tensor": dev["tensor"]}) for q, dev in ((1, xn), (2, yn), (3, diag)) for sec in (s, 1 - s)] + [(0, sib)]

    def sp_sends(l):
        return [remote(sp_in, spv.at[l, q], sp_send.at[i], sp_recv.at[l, q], dev) for i, (q, dev) in enumerate(others)]

    def sp_wait(l):
        for q in range(4):
            pltpu.make_async_copy(spv.at[l, q], spv.at[l, q], sp_recv.at[l, q]).wait()

    loads = [pltpu.make_async_copy(src, dst, pre.at[i]) for i, (src, dst) in enumerate(
        [(wq_in.at[i], wa_in.at[pl.ds(i * HB, HB)]) for i in range(3)] + [(wo_in, wa_in.at[pl.ds(3 * HB, HB)]), (qv_in, qv), (ub_in, ub)] + [(v, vecs.at[i]) for i, v in enumerate((v0_in, v1_in, v2_in, v3_in, v4_in, v5_in))])]
    xcopy = pltpu.make_async_copy(x_in.at[s], xb, loc.at[0])
    for d in loads:
        d.start()
    xcopy.start()
    barrier = pltpu.get_barrier_semaphore()
    for dev in [zn] + [dev for q, dev in others]:
        pl.semaphore_signal(barrier, inc=1, device_id=dev, device_id_type=MESH)
    for d in loads:
        d.wait()
    zeros = jnp.zeros((1, HB), f32)
    sp_in[0:1, :] = jnp.concatenate([ub[i] for i in range(FB // HS)], axis=1)
    sp_in[1:2, :] = jnp.concatenate([qv[i, 0:1, :] for i in range(HPB)] + [zeros] + [qv[i, 1:2, :] for i in range(HPB)] + [zeros], axis=1)
    for i in range(6):
        sp_in[2 + i:3 + i, :] = vecs[i]
    first = (t * 2 + s) * nch
    place = lax.broadcasted_iota(jnp.int32, (1, L), 1)
    for i in range(nch):
        kb_ref[i:i + 1, :] = jnp.where(place < len_ref[first + i], 0.0, MASK_FILL)
    pl.semaphore_wait(barrier, 1 + len(others))

    for l in range(2):
        @pl.when(s == l)
        def _():
            for d in sp_sends(l):
                d.start()
            pltpu.make_async_copy(sp_in, spv.at[l, 0], sp_recv.at[l, 0]).start()
            if l == 0:
                for k in (KA, KU):
                    for d in own_sends(l, k):
                        d.start()
            for k in range(3):
                pltpu.make_async_copy(srcs[k], wv.at[l, k, 0], recv.at[l, k, 0]).start()
                own_local(l, k).start()
    for l in range(2):
        sp_wait(l)
    xcopy.wait()
    spsave = pltpu.make_async_copy(spv, sp_out, loc.at[1])
    spsave.start()

    def saves(l, which):
        pairs = {0: (qkv, qkv_out.at[l]), 1: (a, a_out.at[l]), 2: (c, c_out.at[l]), 3: (u.at[0], u_out.at[l, 0]),
                 4: (inv, inv_out.at[l]), 5: (g, g_out.at[l]), 6: (gp, gp_out.at[l]), 7: (u.at[1], u_out.at[l, 1]), 8: (xb, y_out.at[l])}
        src, dst = pairs[which]
        return pltpu.make_async_copy(src, dst, ssave.at[which])

    def layer(l, _):
        acc[...] = jnp.zeros_like(acc)
        @pl.when(l == 1)
        def _():
            for w in (0, 1, 2):
                saves(0, w).wait()

        def attn_step(r, _):
            @pl.when(r == 0)
            def _():
                arrive(l, KA, 0)
            @pl.when(r == 1)
            def _():
                @pl.when(l == 0)
                def _():
                    arrive(0, KA, 1)
                    arrive(0, KA, 2)
                for k, p in ((KU, 1), (KU, 2), (KA, 5), (KA, 6)):
                    arrive(l, k, p)

            @pl.when(r == 3)
            def _():
                for k, p in ((KA, 3), (KA, 4), (KU, 5), (KU, 6), (KA, 7)):
                    arrive(l, k, p)
            attn_fwd_block(xb, wv.at[l, KA, r], spv.at[l, r], kb_ref, qkv.at[r], a.at[r], c.at[r], acc, nch, L)
            return 0
        lax.fori_loop(0, 4, attn_step, 0)
        arrive(l, KD, 1)
        arrive(l, KD, 2)

        @pl.when((l == 0) & (s == 0))
        def _():
            pl.semaphore_signal(go, inc=1, device_id=sib, device_id_type=MESH)

        @pl.when((l == 0) & (s == 1))
        def _():
            pl.semaphore_wait(go, 1)
            for k in (KA, KU):
                for d in own_sends(1, k):
                    d.start()
        for w in (0, 1, 2):
            saves(l, w).start()
        @pl.when(l == 1)
        def _():
            for w in (3, 4, 5, 6, 7):
                saves(0, w).wait()
        ln1_fwd(xb, acc, spv.at[l, 0], u.at[0], inv.at[0], nlow, rms, M)
        saves(l, 3).start()

        def up_step(r, _):
            @pl.when(r == 0)
            def _():
                arrive(l, KU, 0)

            @pl.when(r == 3)
            def _():
                for k, p in ((KU, 3), (KU, 4), (KD, 5), (KD, 6), (KD, 3), (KD, 4), (KU, 7)):
                    arrive(l, k, p)
            up_block(nlow, wv.at[l, KU, r], spv.at[l, r], g.at[r], gp.at[r])
            return 0
        lax.fori_loop(0, 4, up_step, 0)
        saves(l, 5).start()
        saves(l, 6).start()
        acc[...] = jnp.zeros_like(acc)
        @pl.when(l == 1)
        def _():
            saves(0, 8).wait()

        def down_step(r, _):
            @pl.when(r == 0)
            def _():
                arrive(l, KD, 0)

            @pl.when(r == 3)
            def _():
                arrive(l, KD, 7)

                @pl.when(l == 0)
                def _():
                    arrive(1, KA, 1)
                    arrive(1, KA, 2)
            down_block(g.at[r], wv.at[l, KD, r], acc)
            return 0
        lax.fori_loop(0, 4, down_step, 0)
        ln2_fwd(u.at[0], acc, spv.at[l, 0], u.at[1], inv.at[1], xb, rms, M)
        for w in (4, 7, 8):
            saves(l, w).start()
        for k in range(3):
            for ch in range(nch):
                rs = slice(ch * L, (ch + 1) * L)
                live = lax.broadcasted_iota(jnp.int32, (L, 1), 0) < len_ref[first + ch]
                v = jnp.sum(jnp.where(live, rms[k, rs, :], 0.0), axis=0, keepdims=True)
                rmsv[l, pl.ds(k * nch + ch, 1), :] = jnp.broadcast_to(v, (1, 128))
        return 0
    lax.fori_loop(0, 2, layer, 0)
    for w in range(9):
        saves(1, w).wait()
    rc = pltpu.make_async_copy(rmsv, rms_out, loc.at[0])
    rc.start()
    rc.wait()
    spsave.wait()
    for l in range(2):
        for k in range(3):
            for p in range(8):
                save_w(l, k, p).wait()
        @pl.when(s == l)
        def _():
            for k in range(3):
                for d in own_sends(l, k) + [own_local(l, k), fwd_y(l, k), fwd_x(l, k)] + [to_z(l, k, q) for q in (1, 2, 3)] + [to_sib(l, k, p) for p in range(1, 8)]:
                    d.wait_send()
            for d in sp_sends(l):
                d.wait_send()


def run_k1(nch, L, lengths, x, *ops):
    M = nch * L
    S = jax.ShapeDtypeStruct
    V = pltpu.VMEM
    any_ = pl.BlockSpec(memory_space=pl.ANY)
    outs = (S((2, 3, 4, D, 768), bf16), S((2, 4, 8, D), f32), S((2, 4, M, 3 * HB), bf16), S((2, 4, nch, 3, L, L), bf16), S((2, 4, M, HB), bf16),
            S((2, 2, M, D), f32), S((2, 2, M, 1), f32), S((2, 4, M, FB), bf16), S((2, 4, M, FB), f32), S((2, M, D), bf16), S((2, 16, 128), f32))
    DMA = pltpu.SemaphoreType.DMA
    return pl.pallas_call(
        functools.partial(k1_kernel, nch, L),
        out_shape=outs,
        in_specs=[pl.BlockSpec(memory_space=pltpu.SMEM)] + [any_] * (1 + len(ops)),
        out_specs=[any_] * len(outs),
        scratch_shapes=[V((2, 3, 4, D, 768), bf16), V((2, 4, 8, D), f32), V((M, D), bf16), V((4, M, 3 * HB), bf16), V((4, nch, 3, L, L), bf16), V((4, M, HB), bf16),
                        V((2, M, D), f32), V((2, M, 1), f32), V((4, M, FB), bf16), V((4, M, FB), f32), V((M, D), bf16), V((M, D), f32), V((3, M, 1), f32), V((2, 16, 128), f32),
                        V((D, 768), bf16), V((8, D), f32), V((HPB, 2, HS), f32), V((FB // HS, 1, HS), f32), V((6, 1, D), f32), V((nch, L), f32),
                        DMA((2, 3, 8)), DMA((3, 15)), DMA((2, 4)), DMA((7,)), DMA((2,)), DMA((2, 3, 8)), DMA((9,)), DMA((12,)), pltpu.SemaphoreType.REGULAR],
        compiler_params=pltpu.CompilerParams(collective_id=0, has_side_effects=True, vmem_limit_bytes=62 << 20),
        name="gather_forward",
    )(lengths, x, *ops)

NJ = 4


def k2_kernel(nch, L, n_dp, zin,
              w_in, sp_in, qkv_in, a_in, c_in, u_in, inv_in, g_in, gp_in, y_in, x_in, dy_in, rms_in,
              f_out, sm_out, lo_out, dh_out, rm_out,
              wd, wu, wa, gp, g, qkv, a, c, u, inv, xin, dyv, spv, dx, low, low2, dc, dqkv, xt, xt2,
              pbuf, dbuf, qbuf, xbuf, ybuf, zbuf, fbuf, sm, smr,
              st_g, st_f, st_a, ld, dsend, drecv, xsend, xrecv, ysend, yrecv, zsend, zrecv, fsend, frecv, fl, msend, mrecv, osend, orecv, ol,
              dcred, xcred, ycred):
    M = nch * L
    sub = D // (NJ * 4)
    s = lax.axis_index("section")
    t = lax.axis_index("tensor")
    j = lax.axis_index("dp")
    xn = {"tensor": t + 1 - 2 * lax.rem(t, 2)}
    yn = {"tensor": t + 2 - 4 * lax.rem(t // 2, 2)}
    sib = {"section": 1 - s}
    zn = [{"dp": lax.rem(j + d, n_dp)} for d in range(1, n_dp)] if zin else []

    def remote(src, dst, ss, rs, dev):
        return pltpu.make_async_remote_copy(src_ref=src, dst_ref=dst, send_sem=ss, recv_sem=rs, device_id=dev, device_id_type=MESH)

    def arrived(ref, sem):
        pltpu.make_async_copy(ref, ref, sem).wait()

    def where_of(m):
        li = m // 4
        return 1 - li, 3 - (m - 4 * li), lax.rem(m, 2)

    def g_copies(m):
        l, r, b = where_of(m)
        return [pltpu.make_async_copy(g_in.at[l, r], g.at[b], st_g.at[b])]

    def f_copies(m):
        l, r, b = where_of(m)
        return [pltpu.make_async_copy(w_in.at[l, KD, r], wd.at[b], st_f.at[b, 0]),
                pltpu.make_async_copy(w_in.at[l, KU, r], wu.at[b], st_f.at[b, 1]),
                pltpu.make_async_copy(gp_in.at[l, r], gp.at[b], st_f.at[b, 2])]

    def a_copies(m):
        l, r, b = where_of(m)
        return [pltpu.make_async_copy(w_in.at[l, KA, r], wa.at[b], st_a.at[b, 0]),
                pltpu.make_async_copy(qkv_in.at[l, r], qkv.at[b], st_a.at[b, 1]),
                pltpu.make_async_copy(a_in.at[l, r], a.at[b], st_a.at[b, 2]),
                pltpu.make_async_copy(c_in.at[l, r], c.at[b], st_a.at[b, 3])]

    def begin(copies):
        for d in copies:
            d.start()

    def finish(copies):
        for d in copies:
            d.wait()

    def u_copies(l, i):
        return [pltpu.make_async_copy(u_in.at[l, i], u.at[i], ld.at[2 * i]), pltpu.make_async_copy(inv_in.at[l, i], inv.at[i], ld.at[2 * i + 1])]

    def x_copy(src):
        return [pltpu.make_async_copy(src, xin, ld.at[4])]

    first = [pltpu.make_async_copy(dy_in.at[s], dyv, ld.at[5]), pltpu.make_async_copy(sp_in, spv, ld.at[6])]
    begin(first)
    begin(u_copies(1, 1))
    begin(g_copies(0))
    begin(u_copies(1, 0))
    begin(g_copies(1))
    begin(f_copies(0))
    begin(f_copies(1))
    begin(x_copy(y_in.at[0]))
    begin(a_copies(0))
    begin(a_copies(1))

    barrier = pltpu.get_barrier_semaphore()
    for dev in [xn, yn, sib] + zn:
        pl.semaphore_signal(barrier, inc=1, device_id=dev, device_id_type=MESH)
    pl.semaphore_wait(barrier, 3 + len(zn))

    def out_send(src, dst, i):
        return remote(src.at[1 - s], dst.at[s], osend.at[i], orecv.at[i], sib)

    def out_keep(src, dst, i):
        return pltpu.make_async_copy(src.at[s], dst.at[s], ol.at[i])
    for src, dst, i in ((y_in, lo_out, 0), (rms_in, rm_out, 1)):
        out_send(src, dst, i).start()
        out_keep(src, dst, i).start()

    def d_copy(r):
        return remote(pbuf.at[r, 1 - s], dbuf.at[r], dsend.at[r], drecv.at[r], sib)

    def put(n, r, parts):
        @pl.when(n > 0)
        def _():
            d_copy(r).wait_send()
        for k in range(NJ):
            for h in range(2):
                for ab in range(2):
                    lo = ((k * 2 + h) * 2 + ab) * sub
                    pbuf[r, h, ab, k] = parts[lo:lo + sub, :].astype(bf16)

        @pl.when(n > 0)
        def _():
            pl.semaphore_wait(dcred, 1)
        d_copy(r).start()

    def x_copies(n):
        b = lax.rem(n, 3)
        return [remote(qbuf.at[n, 0, 3], xbuf.at[b, 1], xsend.at[n, 1], xrecv.at[n, 1], xn),
                remote(qbuf.at[n, 1, 3], xbuf.at[b, 3], xsend.at[n, 3], xrecv.at[n, 3], yn),
                remote(qbuf.at[n, 1, 2], xbuf.at[b, 2], xsend.at[n, 2], xrecv.at[n, 2], yn),
                remote(qbuf.at[n, 0, 1], xbuf.at[b, 0], xsend.at[n, 0], xrecv.at[n, 0], xn)]

    def d_add(n, r):
        arrived(dbuf.at[r], drecv.at[r])

        def one(ab, _):
            qbuf[n, ab, r] = (pbuf[r, s, ab].astype(f32) + dbuf[r, ab].astype(f32)).astype(bf16)
            return 0
        lax.fori_loop(0, 2, one, 0)

        @pl.when(n < 5)
        def _():
            pl.semaphore_signal(dcred, inc=1, device_id=sib, device_id_type=MESH)
        cs = x_copies(n)

        @pl.when(r == 3)
        def _():
            @pl.when(n >= 3)
            def _():
                pl.semaphore_wait(xcred, 1)
                pl.semaphore_wait(ycred, 1)
            cs[0].start()
            cs[1].start()

        @pl.when(r == 2)
        def _():
            cs[2].start()

        @pl.when(r == 1)
        def _():
            cs[3].start()

    def slots(n, step):
        def body(ri, _):
            step(ri, 3 - ri)

            @pl.when(ri > 0)
            def _():
                d_add(n, 4 - ri)
            return 0
        lax.fori_loop(0, 4, body, 0)
        d_add(n, 0)

    def y_copies(n):
        return [remote(qbuf.at[n, 0, 2], ybuf.at[n, 0], ysend.at[n, 0], yrecv.at[n, 0], yn),
                remote(qbuf.at[n, 1, 1], ybuf.at[n, 1], ysend.at[n, 1], yrecv.at[n, 1], xn)]

    def add_to(n, ab, r, ref):
        qbuf[n, ab, r] = (qbuf[n, ab, r].astype(f32) + ref[...].astype(f32)).astype(bf16)

    def ev_x(n):
        b = lax.rem(n, 3)
        arrived(xbuf.at[b, 1], xrecv.at[n, 1])
        add_to(n, 0, 2, xbuf.at[b, 1])
        cs = y_copies(n)
        cs[0].start()
        arrived(xbuf.at[b, 3], xrecv.at[n, 3])
        add_to(n, 1, 1, xbuf.at[b, 3])
        cs[1].start()
        arrived(xbuf.at[b, 0], xrecv.at[n, 0])
        add_to(n, 0, 0, xbuf.at[b, 0])
        arrived(xbuf.at[b, 2], xrecv.at[n, 2])
        add_to(n, 1, 0, xbuf.at[b, 2])

        @pl.when(n < 3)
        def _():
            pl.semaphore_signal(xcred, inc=1, device_id=xn, device_id_type=MESH)
            pl.semaphore_signal(ycred, inc=1, device_id=yn, device_id_type=MESH)

    def z_copies(n):
        return [remote(qbuf.at[n, :, 0, lax.rem(j + d, n_dp)], zbuf.at[n, d - 1], zsend.at[n, d - 1], zrecv.at[n, d - 1], zn[d - 1]) for d in range(1, n_dp)]

    def q_copy(n):
        li = n // 3
        return pltpu.make_async_copy(qbuf.at[n, :, 0], f_out.at[1 - li, 2 - (n - 3 * li)], fl.at[n])

    def ev_y(n):
        for i in range(2):
            arrived(ybuf.at[n, i], yrecv.at[n, i])
            add_to(n, i, 0, ybuf.at[n, i])
        if zin:
            begin(z_copies(n))
        else:
            q_copy(n).start()

    def f_keep(n):
        return pltpu.make_async_copy(fbuf.at[n], f_out.at[2 - lax.rem(n, 3), s], fl.at[lax.rem(n, 3)])

    def f_send(n):
        return remote(fbuf.at[n], f_out.at[2 - lax.rem(n, 3), s], fsend.at[lax.rem(n, 3)], frecv.at[lax.rem(n, 3)], sib)

    def ev_z(n):
        if not zin:
            return
        tot = qbuf[n, :, 0, j].astype(f32)
        for d in range(n_dp - 1):
            arrived(zbuf.at[n, d], zrecv.at[n, d])
            tot = tot + zbuf[n, d].astype(f32)
        fbuf[n] = tot
        mine = (1 - n // 3) == s

        @pl.when(mine)
        def _():
            f_keep(n).start()

        @pl.when(jnp.logical_not(mine))
        def _():
            f_send(n).start()

    def m_copy(i):
        if i == 0:
            return remote(sm.at[1 - s], smr.at[0], msend.at[0], mrecv.at[0], sib)
        return remote(sm.at[s], smr.at[i], msend.at[i], mrecv.at[i], xn if i == 1 else yn)

    def m_z(d):
        return remote(sm.at[s], smr.at[2 + d], msend.at[2 + d], mrecv.at[2 + d], zn[d - 1])

    def m_add(i, flip):
        arrived(smr.at[i], mrecv.at[i])
        if i in (1, 2):
            m_copy(i).wait_send()
        sm[s, 0:8, :] += smr[i, 0:8, :]
        for r in range(4):
            for base in (8, 12):
                sm[s, base + r:base + r + 1, :] += smr[i, base + (r ^ flip):base + (r ^ flip) + 1, :]

    finish(first)
    sm[...] = jnp.zeros_like(sm)

    def layer(li, _):
        l = 1 - li
        n0 = 3 * li
        spl = spv.at[l, 0]
        sml = sm.at[l]
        finish(u_copies(l, 1))
        norm_bwd(dyv, u.at[1], inv.at[1], spl[6:7, :], dx, low, sml, 3, M)

        @pl.when(li == 0)
        def _():
            begin(u_copies(0, 1))
        xt[...] = low[...].T

        def down_step(ri, r):
            m = 4 * li + ri
            finish(g_copies(m))
            put(n0, r, dot(xt[...], g[lax.rem(m, 2)]))

            @pl.when(m + 2 < 8)
            def _():
                begin(g_copies(m + 2))
        slots(n0, down_step)

        @pl.when(li == 1)
        def _():
            ev_y(1)
        finish(u_copies(l, 0))
        low2[...] = (u[0] * spl[3:4, :] + spl[4:5, :]).astype(bf16)
        xt[...] = low2[...].T

        def up_step(ri, r):
            m = 4 * li + ri
            b = lax.rem(m, 2)
            finish(f_copies(m))
            ffn_bwd_block(low, wu.at[b], wd.at[b], gp.at[b], low2, dx, sml.at[pl.ds(8 + r, 1)])
            put(n0 + 1, r, dot(xt[...], low2[...]))

            @pl.when(m + 2 < 8)
            def _():
                begin(f_copies(m + 2))
        slots(n0 + 1, up_step)

        @pl.when(li == 1)
        def _():
            ev_x(2)
            ev_z(0)
        norm_bwd(dx, u.at[0], inv.at[0], spl[3:4, :], dx, low, sml, 0, M)

        @pl.when(li == 0)
        def _():
            begin(u_copies(0, 0))
        xt2[...] = low[...].T
        finish(x_copy(x_in.at[s]))
        xt[...] = xin[...].T

        @pl.when(li == 0)
        def _():
            begin(x_copy(x_in.at[s]))

        def attn_step(ri, r):
            m = 4 * li + ri
            b = lax.rem(m, 2)
            finish(a_copies(m))
            attn_bwd_block(low, wa.at[b], qkv.at[b], a.at[b], dc, dqkv, dx, sml.at[pl.ds(12 + r, 1)], nch, L)
            put(n0 + 2, r, jnp.concatenate([dot(xt[...], dqkv[...]), dot(xt2[...], c[b])], axis=1))

            @pl.when(m + 2 < 8)
            def _():
                begin(a_copies(m + 2))

            @pl.when((li == 0) & (ri == 1))
            def _():
                ev_x(0)

            @pl.when((li == 0) & (ri == 3))
            def _():
                ev_x(1)
                ev_y(0)

            @pl.when((li == 1) & (ri == 3))
            def _():
                ev_x(3)
        slots(n0 + 2, attn_step)
        dyv[...] = dx[...].astype(bf16)
        own = l == s

        @pl.when(own)
        def _():
            dh_keep().start()

        @pl.when(jnp.logical_not(own))
        def _():
            dh_send().start()

        @pl.when(own & (li == 0))
        def _():
            dh_keep().wait()

        @pl.when(jnp.logical_not(own) & (li == 0))
        def _():
            dh_send().wait_send()
        return 0

    def dh_keep():
        return pltpu.make_async_copy(dyv, dh_out.at[s], ol.at[2])

    def dh_send():
        return remote(dyv, dh_out.at[s], osend.at[2], orecv.at[2], sib)

    lax.fori_loop(0, 2, layer, 0)

    m_copy(0).start()
    ev_y(2)
    m_add(0, 0)
    m_copy(1).start()
    ev_z(1)
    ev_x(4)
    m_add(1, 1)
    m_copy(2).start()
    ev_y(3)
    ev_z(2)
    m_add(2, 2)
    if zin:
        for d in range(1, n_dp):
            m_z(d).start()
    ev_x(5)
    ev_y(4)
    ev_z(3)
    ev_y(5)
    ev_z(4)
    if zin:
        for d in range(1, n_dp):
            m_z(d).wait_send()
        for d in range(1, n_dp):
            m_add(2 + d, 0)
    smc = pltpu.make_async_copy(sm.at[s], sm_out, ld.at[5])
    smc.start()
    ev_z(5)

    smc.wait()
    m_copy(0).wait_send()
    for r in range(4):
        d_copy(r).wait_send()
    for n in range(6):
        for d in x_copies(n) + y_copies(n):
            d.wait_send()
        if zin:
            for d in z_copies(n):
                d.wait_send()
        else:
            q_copy(n).wait()
    for src, dst, i in ((y_in, lo_out, 0), (rms_in, rm_out, 1)):
        out_send(src, dst, i).wait()
        out_keep(src, dst, i).wait()
    @pl.when(s == 0)
    def _():
        dh_keep().wait()
    @pl.when(s == 1)
    def _():
        dh_send().wait_send()
    arrived(dh_out.at[1 - s], orecv.at[2])
    if zin:
        for k in range(3):
            arrived(f_out.at[2 - k, 1 - s], frecv.at[k])
            f_keep(k).wait()
            f_send(k).wait_send()


def run_k2(nch, L, n_dp, *ops):
    M = nch * L
    zin = n_dp == 4
    sub = D // (NJ * 4)
    S = jax.ShapeDtypeStruct
    V = pltpu.VMEM
    any_ = pl.BlockSpec(memory_space=pl.ANY)
    outs = (S((3, 2, 2, sub, 768), f32) if zin else S((2, 3, 2, NJ, sub, 768), bf16), S((16, 768), f32), S((2, M, D), bf16), S((2, M, D), bf16), S((2, 16, 128), f32))
    DMA = pltpu.SemaphoreType.DMA
    REG = pltpu.SemaphoreType.REGULAR
    bufs = [V((2, D, 768), bf16), V((2, D, 768), bf16), V((2, D, 768), bf16), V((2, M, FB), f32), V((2, M, FB), bf16), V((2, M, 3 * HB), bf16), V((2, nch, HPB, L, L), bf16), V((2, M, HB), bf16),
            V((2, M, D), f32), V((2, M, 1), f32), V((M, D), bf16), V((M, D), bf16), V((2, 4, 8, D), f32), V((M, D), f32), V((M, D), bf16), V((M, D), bf16), V((M, HB), bf16), V((M, 3 * HB), bf16), V((D, M), bf16), V((D, M), bf16),
            V((4, 2, 2, NJ, sub, 768), bf16), V((4, 2, NJ, sub, 768), bf16), V((6, 2, 4, NJ, sub, 768), bf16), V((3, 4, NJ, sub, 768), bf16), V((6, 2, NJ, sub, 768), bf16),
            V((6, 3, 2, sub, 768) if zin else (8, 128), bf16), V((6, 2, sub, 768) if zin else (8, 128), f32), V((2, 16, 768), f32), V((6, 16, 768), f32)]
    sems = [DMA((2,)), DMA((2, 3)), DMA((2, 4)), DMA((7,)), DMA((4,)), DMA((4,)), DMA((6, 4)), DMA((6, 4)), DMA((6, 2)), DMA((6, 2)), DMA((6, 3)), DMA((6, 3)), DMA((3,)), DMA((3,)), DMA((6,)), DMA((6,)), DMA((6,)),
            DMA((3,)), DMA((3,)), DMA((3,)), REG, REG, REG]
    return pl.pallas_call(
        functools.partial(k2_kernel, nch, L, n_dp, zin),
        out_shape=outs,
        in_specs=[any_] * 13,
        out_specs=[any_] * len(outs),
        scratch_shapes=bufs + sems,
        compiler_params=pltpu.CompilerParams(collective_id=1, has_side_effects=True, vmem_limit_bytes=63 << 20),
        name="backward_reduce",
    )(*ops)

def finish_kernel(n_dp, nch, len_ref, f_in, sm_in, rm_in, lo_in, dh_in, lo_out, dh_out, gu, gd, gq, qb, go, ub, vec, sums, f_ref, sm_ref, rm_ref, lo_ref, dh_ref, sem):
    t = lax.axis_index("tensor")
    j = lax.axis_index("dp")
    loads = [pltpu.make_async_copy(src, dst, sem.at[i]) for i, (src, dst) in enumerate(((f_in, f_ref), (sm_in, sm_ref), (rm_in, rm_ref), (lo_in, lo_ref), (dh_in, dh_ref)))]
    stores = [pltpu.make_async_copy(src, dst, sem.at[5 + i]) for i, (src, dst) in enumerate(((f_ref.at[1], gu), (f_ref.at[2], gd), (lo_ref, lo_out), (dh_ref, dh_out)))]
    for d in loads:
        d.start()
    for d in loads:
        d.wait()
    for d in stores:
        d.start()
    ga = f_ref[0]
    for i in range(3):
        gq[i] = ga[:, i * HB:(i + 1) * HB]
    go[...] = ga[:, 3 * HB:4 * HB].T
    part = HS // n_dp
    share = D // (4 * n_dp)
    off = (j * 4 + t) * share
    rolled = pltpu.roll(sm_ref[0:8, :], lax.rem(D - off, D), 1)
    for i in range(6):
        vec[i] = rolled[i:i + 1, 0:share]
    slots = pltpu.roll(sm_ref[8:16, :], lax.rem(D - j * part, D), 1)
    for i in range(FB // HS):
        ub[i] = slots[0:1, i * HS:i * HS + part]
    for i in range(HPB):
        for b in range(2):
            lo = 2 * b * HB + i * HS
            qb[i, b:b + 1, :] = slots[4:5, lo:lo + part]
    for h in range(2):
        for c in range(nch):
            at = h * nch + c
            size = len_ref[t * 2 * nch + at].astype(f32)
            for k in range(3):
                sums[k, 0:1, at:at + 1] = rm_ref[h, k * nch + c:k * nch + c + 1, 0:1] / size
    for d in stores:
        d.wait()


def run_finish(n_dp, nch, M, lengths, f, sm, rm, lo, dh):
    S = jax.ShapeDtypeStruct
    V = pltpu.VMEM
    dd = D // n_dp
    part = HS // n_dp
    vm = pl.BlockSpec(memory_space=pltpu.VMEM)
    any_ = pl.BlockSpec(memory_space=pl.ANY)
    return pl.pallas_call(
        functools.partial(finish_kernel, n_dp, nch),
        out_shape=(S((2, M, D), bf16), S((2, M, D), bf16), S((dd, FB), f32), S((dd, FB), f32), S((3, dd, HB), f32), S((HPB, 2, part), f32), S((HB, dd), f32),
                   S((FB // HS, 1, part), f32), S((6, 1, D // (4 * n_dp)), f32), S((3, 1, 2 * nch), f32)),
        in_specs=[pl.BlockSpec(memory_space=pltpu.SMEM)] + [any_] * 5,
        out_specs=[any_] * 4 + [vm] * 6,
        scratch_shapes=[V((3, dd, FB), f32), V((16, D), f32), V((2, 16, 128), f32), V((2, M, D), bf16), V((2, M, D), bf16), pltpu.SemaphoreType.DMA((9,))],
        compiler_params=pltpu.CompilerParams(vmem_limit_bytes=60 << 20),
        name="finish",
    )(lengths, f, sm, rm, lo, dh)


def on_device(inputs, lengths, cotangent, w_qkv, qv_bias, w_out, out_bias, ln1_gain, ln1_bias, w_up, up_bias, w_down, down_bias, ln2_gain, ln2_bias):
    s = lax.axis_index("section")
    n_dp = lax.axis_size("dp")
    chains, L, _ = inputs.shape
    nch = chains // 2
    M = nch * L
    x = inputs.reshape(2, M, D)
    dy = cotangent.reshape(2, M, D)
    w_all, sp_all, qkv, a, c, u, inv, g, gp, y, rms = run_k1(
        nch, L, lengths, x, jnp.swapaxes(w_qkv[0], 1, 2), w_out[0], w_up[0], w_down[0], qv_bias[0].transpose(1, 0, 2), up_bias.transpose(1, 0, 2), out_bias, ln1_gain, ln1_bias, down_bias, ln2_gain, ln2_bias)
    grads, sm, lo, dh, rm = run_k2(nch, L, n_dp, w_all, sp_all, qkv, a, c, u, inv, g, gp, y, x, dy, rms)
    if n_dp == 4:
        grads = grads.reshape(3, D // n_dp, 768)
    else:
        mine = grads[s].astype(f32)
        got = lax.ppermute(grads[1 - s], "section", [(0, 1), (1, 0)]).astype(f32)
        both = jnp.stack([jnp.where(s == 0, mine, got), jnp.where(s == 0, got, mine)])
        both = both.transpose(1, 3, 0, 2, 4, 5).reshape(3, D, 768)
        grads = lax.psum_scatter(both, "dp", scatter_dimension=1, tiled=True)
        sm = lax.psum(sm, "dp")
    lo, dh, gu, gd, gq, qb, go, ub, vec, sums = run_finish(n_dp, nch, M, lengths, grads, sm, rm, lo, dh)
    return (lo.reshape(1, chains, L, D), dh.reshape(1, chains, L, D), gq[None], qb.transpose(1, 0, 2)[None], go[None], gu[None],
            ub.transpose(1, 0, 2), gd.T[None], vec.transpose(1, 0, 2), sums.transpose(1, 0, 2))


def solution(mesh):
    in_specs = (
        P(("dp", "tensor"), None, None),
        P("dp"),
        P(("dp", "tensor"), None, None),
        P("section", None, None, "tensor"),
        P("section", None, "tensor", None),
        P("section", "tensor", None),
        P("section", None),
        P("section", None),
        P("section", None),
        P("section", None, "tensor"),
        P("section", "tensor", None),
        P("section", "tensor", None),
        P("section", None),
        P("section", None),
        P("section", None),
    )
    out_specs = (
        P("section", ("dp", "tensor"), None, None),
        P("section", ("dp", "tensor"), None, None),
        P("section", None, "dp", "tensor"),
        P("section", None, "tensor", "dp"),
        P("section", "tensor", "dp"),
        P("section", "dp", "tensor"),
        P("section", "tensor", "dp"),
        P("section", "tensor", "dp"),
        P("section", None, ("dp", "tensor")),
        P("section", None, ("dp", "tensor")),
    )
    return jax.shard_map(on_device, mesh=mesh, in_specs=in_specs, out_specs=out_specs, check_vma=False)
```

profile of v0, /device:TPU:0, one launch (start us, length us, event | category | flops | bytes accessed | tf_op | source)
XLA Modules:
  0.0 271.5 jit_solution(3286783482214669524)
XLA Ops:
  0.6 106.8 %gather_forward.1 = (bf16[2,3,4,768,768]{4,3,2,1,0:T(8,128)(2,1)}, f32[2,4,8,768]{3,2,1,0:T(8,128)}, bf16[2,4,480,576]{3,2,1,0:T(8,128)(2,1)}, bf16[2,4,3,3,160,...) custom-call(s32[24]{0:T(128)} %len_ref.3, ...), custom_call_target="tpu_custom_call" | custom-call | tf_op jit(solution)/shard_map/gather_forward/pallas_call | solution.py:456
  107.5 157.8 %backward_reduce.1 = (f32[3,2,2,48,768]{4,3,2,1,0:T(8,128)}, f32[16,768]{1,0:T(8,128)}, bf16[2,480,768]{2,1,0:T(8,128)(2,1)}, bf16[2,480,768]{2,1,0:T(8,128)(2,1)}, f32[2,16,128]{2,1,0:T(8,128)}) custom-call(bf16[2,3,4,768,768]{4,3,2,1,0:T(8,128)(2,1)} %get-tuple-element.36.w_in, f32[2,4,8,768]{3,2,1,0:T(8,128)} %get-tuple-element.37.sp_in, ...), custom_call_target="tpu_custom_call" | custom-call | tf_op jit(solution)/shard_map/backward_reduce/pallas_call | solution.py:892
  265.3 6.0 %finish.1 = (bf16[2,480,768]{2,1,0:T(8,128)(2,1)}, bf16[2,480,768]{2,1,0:T(8,128)(2,1)}, f32[192,768]{1,0:T(8,128)}, f32[192,768]{1,0:T(8,128)}, f32[3,192,192]{...) custom-call(s32[24]{0:T(128)} %len_ref.3, ...), custom_call_target="tpu_custom_call" | custom-call | tf_op jit(solution)/shard_map/finish/pallas_call | solution.py:947
where the time goes:
time: 273 us; the launch traced here: 271 us
  Pallas kernels  271 us (99%)
    pallas_call x1, Pallas kernels, run_k2(): pl.pallas_call(functools.partial(k2_kernel, nch, L, n_dp, zin), out_shape...  158 us
    pallas_call x1, Pallas kernels, run_k1(): pl.pallas_call(functools.partial(k1_kernel, nch, L), out_shape=outs, in_s...  107 us
    pallas_call x1, Pallas kernels, run_finish(): pl.pallas_call(functools.partial(finish_kernel, n_dp, nch), out_shape=(S(...  6.01 us

commit v1 on v0

--- a/solution.py
+++ b/solution.py
@@ -183,7 +183,7 @@
         dqkv_ref[rs, :] = jnp.concatenate(dqs + dks + dvs, axis=1).astype(bf16)
     dx_ref[...] += dot(dqkv_ref[...], wa_ref[0:3 * HB, :])
     qb_ref[:, 0:3 * HB] = col_sum(dqkv_ref[...].astype(f32))
-ZR = 224
+ZR = 192
 XY = D - ZR
 
 
@@ -267,6 +267,11 @@
                 if k == KA:
                     for d in own_sends(l, KD):
                         d.start()
+
+                    @pl.when(l == 0)
+                    def _():
+                        own_local(0, KU).start()
+                        own_local(0, KD).start()
             if p in (3, 4):
                 @pl.when(e == p - 3)
                 def _():
@@ -318,7 +323,8 @@
                         d.start()
             for k in range(3):
                 pltpu.make_async_copy(srcs[k], wv.at[l, k, 0], recv.at[l, k, 0]).start()
-                own_local(l, k).start()
+                if l == 1 or k == KA:
+                    own_local(l, k).start()
     for l in range(2):
         sp_wait(l)
     xcopy.wait()
@@ -467,13 +473,15 @@
     )(lengths, x, *ops)
 
 NJ = 4
+NC = 2
+CW = 768 // NC
 
 
 def k2_kernel(nch, L, n_dp, zin,
               w_in, sp_in, qkv_in, a_in, c_in, u_in, inv_in, g_in, gp_in, y_in, x_in, dy_in, rms_in,
               f_out, sm_out, lo_out, dh_out, rm_out,
               wd, wu, wa, gp, g, qkv, a, c, u, inv, xin, dyv, spv, dx, low, low2, dc, dqkv, xt, xt2,
-              pbuf, dbuf, qbuf, xbuf, ybuf, zbuf, fbuf, sm, smr,
+              pbuf, dbuf, qbuf, xbuf, ybuf, zbuf, fbuf, sm, smr, z0, x0, y0, z0send, z0recv,
               st_g, st_f, st_a, ld, dsend, drecv, xsend, xrecv, ysend, yrecv, zsend, zrecv, fsend, frecv, fl, msend, mrecv, osend, orecv, ol,
               dcred, xcred, ycred):
     M = nch * L
@@ -542,17 +550,12 @@
     barrier = pltpu.get_barrier_semaphore()
     for dev in [xn, yn, sib] + zn:
         pl.semaphore_signal(barrier, inc=1, device_id=dev, device_id_type=MESH)
-    pl.semaphore_wait(barrier, 3 + len(zn))
 
     def out_send(src, dst, i):
         return remote(src.at[1 - s], dst.at[s], osend.at[i], orecv.at[i], sib)
 
     def out_keep(src, dst, i):
         return pltpu.make_async_copy(src.at[s], dst.at[s], ol.at[i])
-    for src, dst, i in ((y_in, lo_out, 0), (rms_in, rm_out, 1)):
-        out_send(src, dst, i).start()
-        out_keep(src, dst, i).start()
-
     def d_copy(r):
         return remote(pbuf.at[r, 1 - s], dbuf.at[r], dsend.at[r], drecv.at[r], sib)
 
@@ -571,42 +574,50 @@
             pl.semaphore_wait(dcred, 1)
         d_copy(r).start()
 
-    def x_copies(n):
-        b = lax.rem(n, 3)
-        return [remote(qbuf.at[n, 0, 3], xbuf.at[b, 1], xsend.at[n, 1], xrecv.at[n, 1], xn),
-                remote(qbuf.at[n, 1, 3], xbuf.at[b, 3], xsend.at[n, 3], xrecv.at[n, 3], yn),
-                remote(qbuf.at[n, 1, 2], xbuf.at[b, 2], xsend.at[n, 2], xrecv.at[n, 2], yn),
-                remote(qbuf.at[n, 0, 1], xbuf.at[b, 0], xsend.at[n, 0], xrecv.at[n, 0], xn)]
+    def x_copy_of(n, h, i):
+        ab, r, dev = ((0, 1, xn), (0, 3, xn), (1, 2, yn), (1, 3, yn))[i]
+        return remote(qbuf.at[n, h, ab, r], xbuf.at[lax.rem(n, 3), h, i], xsend.at[n, h, i], xrecv.at[n, h, i], dev)
+
+    def cols(h):
+        return slice(h * CW, (h + 1) * CW)
 
     def d_add(n, r):
         arrived(dbuf.at[r], drecv.at[r])
 
         def one(ab, _):
-            qbuf[n, ab, r] = (pbuf[r, s, ab].astype(f32) + dbuf[r, ab].astype(f32)).astype(bf16)
+            for h in range(NC):
+                qbuf[n, h, ab, r] = (pbuf[r, s, ab, :, :, cols(h)].astype(f32) + dbuf[r, ab, :, :, cols(h)].astype(f32)).astype(bf16)
             return 0
         lax.fori_loop(0, 2, one, 0)
 
         @pl.when(n < 5)
         def _():
             pl.semaphore_signal(dcred, inc=1, device_id=sib, device_id_type=MESH)
-        cs = x_copies(n)
-
-        @pl.when(r == 3)
-        def _():
-            @pl.when(n >= 3)
+
+        x_sends(n, r)
+
+    def x_sends(n, r):
+        go = n >= (1 if zin else 0)
+
+        @pl.when(go & (r == 3))
+        def _():
+            @pl.when(n >= (4 if zin else 3))
             def _():
                 pl.semaphore_wait(xcred, 1)
                 pl.semaphore_wait(ycred, 1)
-            cs[0].start()
-            cs[1].start()
-
-        @pl.when(r == 2)
-        def _():
-            cs[2].start()
-
-        @pl.when(r == 1)
-        def _():
-            cs[3].start()
+            for h in range(NC):
+                x_copy_of(n, h, 1).start()
+                x_copy_of(n, h, 3).start()
+
+        @pl.when(go & (r == 2))
+        def _():
+            for h in range(NC):
+                x_copy_of(n, h, 2).start()
+
+        @pl.when(go & (r == 1))
+        def _():
+            for h in range(NC):
+                x_copy_of(n, h, 0).start()
 
     def slots(n, step):
         def body(ri, _):
@@ -619,71 +630,116 @@
         lax.fori_loop(0, 4, body, 0)
         d_add(n, 0)
 
-    def y_copies(n):
-        return [remote(qbuf.at[n, 0, 2], ybuf.at[n, 0], ysend.at[n, 0], yrecv.at[n, 0], yn),
-                remote(qbuf.at[n, 1, 1], ybuf.at[n, 1], ysend.at[n, 1], yrecv.at[n, 1], xn)]
-
-    def add_to(n, ab, r, ref):
-        qbuf[n, ab, r] = (qbuf[n, ab, r].astype(f32) + ref[...].astype(f32)).astype(bf16)
-
-    def ev_x(n):
+    def y_copies(n, h):
+        return [remote(qbuf.at[n, h, 0, 2], ybuf.at[n, h, 0], ysend.at[n, h, 0], yrecv.at[n, h, 0], yn),
+                remote(qbuf.at[n, h, 1, 1], ybuf.at[n, h, 1], ysend.at[n, h, 1], yrecv.at[n, h, 1], xn)]
+
+    def add_to(n, h, ab, r, ref):
+        qbuf[n, h, ab, r] = (qbuf[n, h, ab, r].astype(f32) + ref[...].astype(f32)).astype(bf16)
+
+    def ev_x(n, h):
         b = lax.rem(n, 3)
-        arrived(xbuf.at[b, 1], xrecv.at[n, 1])
-        add_to(n, 0, 2, xbuf.at[b, 1])
-        cs = y_copies(n)
-        cs[0].start()
-        arrived(xbuf.at[b, 3], xrecv.at[n, 3])
-        add_to(n, 1, 1, xbuf.at[b, 3])
-        cs[1].start()
-        arrived(xbuf.at[b, 0], xrecv.at[n, 0])
-        add_to(n, 0, 0, xbuf.at[b, 0])
-        arrived(xbuf.at[b, 2], xrecv.at[n, 2])
-        add_to(n, 1, 0, xbuf.at[b, 2])
-
-        @pl.when(n < 3)
-        def _():
-            pl.semaphore_signal(xcred, inc=1, device_id=xn, device_id_type=MESH)
-            pl.semaphore_signal(ycred, inc=1, device_id=yn, device_id_type=MESH)
-
-    def z_copies(n):
-        return [remote(qbuf.at[n, :, 0, lax.rem(j + d, n_dp)], zbuf.at[n, d - 1], zsend.at[n, d - 1], zrecv.at[n, d - 1], zn[d - 1]) for d in range(1, n_dp)]
-
-    def q_copy(n):
+        cs = y_copies(n, h)
+        for i, ab, r in ((1, 0, 2), (3, 1, 1), (0, 0, 0), (2, 1, 0)):
+            arrived(xbuf.at[b, h, i], xrecv.at[n, h, i])
+            add_to(n, h, ab, r, xbuf.at[b, h, i])
+            if i in (1, 3):
+                cs[i // 2].start()
+        if h == NC - 1:
+            @pl.when((n < 3) & (n > 0) if zin else n < 3)
+            def _():
+                pl.semaphore_signal(xcred, inc=1, device_id=xn, device_id_type=MESH)
+                pl.semaphore_signal(ycred, inc=1, device_id=yn, device_id_type=MESH)
+
+    def z_copies(n, h):
+        return [remote(qbuf.at[n, h, :, 0, lax.rem(j + d, n_dp)], zbuf.at[n, h, d - 1], zsend.at[n, h, d - 1], zrecv.at[n, h, d - 1], zn[d - 1]) for d in range(1, n_dp)]
+
+    def q_copy(n, h):
         li = n // 3
-        return pltpu.make_async_copy(qbuf.at[n, :, 0], f_out.at[1 - li, 2 - (n - 3 * li)], fl.at[n])
-
-    def ev_y(n):
+        return pltpu.make_async_copy(qbuf.at[n, h, :, 0], f_out.at[1 - li, 2 - (n - 3 * li), h], fl.at[n, h])
+
+    def ev_y(n, h):
         for i in range(2):
-            arrived(ybuf.at[n, i], yrecv.at[n, i])
-            add_to(n, i, 0, ybuf.at[n, i])
+            arrived(ybuf.at[n, h, i], yrecv.at[n, h, i])
+            add_to(n, h, i, 0, ybuf.at[n, h, i])
         if zin:
-            begin(z_copies(n))
+            begin(z_copies(n, h))
         else:
-            q_copy(n).start()
+            q_copy(n, h).start()
 
     def f_keep(n):
-        return pltpu.make_async_copy(fbuf.at[n], f_out.at[2 - lax.rem(n, 3), s], fl.at[lax.rem(n, 3)])
+        return pltpu.make_async_copy(fbuf.at[n], f_out.at[2 - lax.rem(n, 3), s], fl.at[lax.rem(n, 3), 0])
 
     def f_send(n):
         return remote(fbuf.at[n], f_out.at[2 - lax.rem(n, 3), s], fsend.at[lax.rem(n, 3)], frecv.at[lax.rem(n, 3)], sib)
 
-    def ev_z(n):
+    def ship(n):
+        mine = (1 - n // 3) == s
+
+        @pl.when(mine)
+        def _():
+            f_keep(n).start()
+
+        @pl.when(jnp.logical_not(mine))
+        def _():
+            f_send(n).start()
+
+    def ev_z(n, h):
         if not zin:
             return
-        tot = qbuf[n, :, 0, j].astype(f32)
+        tot = qbuf[n, h, :, 0, j].astype(f32)
         for d in range(n_dp - 1):
-            arrived(zbuf.at[n, d], zrecv.at[n, d])
-            tot = tot + zbuf[n, d].astype(f32)
-        fbuf[n] = tot
-        mine = (1 - n // 3) == s
-
-        @pl.when(mine)
-        def _():
-            f_keep(n).start()
-
-        @pl.when(jnp.logical_not(mine))
-        def _():
-            f_send(n).start()
+            arrived(zbuf.at[n, h, d], zrecv.at[n, h, d])
+            tot = tot + zbuf[n, h, d].astype(f32)
+        fbuf[n, :, :, cols(h)] = tot
+        if h < NC - 1:
+            return
+        ship(n)
+
+    def first_z(h):
+        return [remote(qbuf.at[0, h, :, :, lax.rem(j + d, n_dp)], z0.at[h, d - 1], z0send.at[h, d - 1], z0recv.at[h, d - 1], zn[d - 1]) for d in range(1, n_dp)]
+
+    def first_x(h, i):
+        ab, r, dev = ((0, 1, xn), (0, 3, xn), (1, 2, yn), (1, 3, yn))[i]
+        return remote(qbuf.at[0, h, ab, r, j], x0.at[h, i], xsend.at[0, h, i], xrecv.at[0, h, i], dev)
+
+    def first_y(h):
+        return [remote(qbuf.at[0, h, 0, 2, j], y0.at[h, 0], ysend.at[0, h, 0], yrecv.at[0, h, 0], yn),
+                remote(qbuf.at[0, h, 1, 1, j], y0.at[h, 1], ysend.at[0, h, 1], yrecv.at[0, h, 1], xn)]
+
+    def add_first(h, ab, r, ref):
+        qbuf[0, h, ab, r, j] = (qbuf[0, h, ab, r, j].astype(f32) + ref[...].astype(f32)).astype(bf16)
+
+    def ev_first_z():
+        for h in range(NC):
+            for d in range(n_dp - 1):
+                arrived(z0.at[h, d], z0recv.at[h, d])
+            for ab in range(2):
+                for r in range(4):
+                    tot = qbuf[0, h, ab, r, j].astype(f32)
+                    for d in range(n_dp - 1):
+                        tot = tot + z0[h, d, ab, r].astype(f32)
+                    qbuf[0, h, ab, r, j] = tot.astype(bf16)
+            for i in range(4):
+                first_x(h, i).start()
+
+    def ev_first_x():
+        for h in range(NC):
+            for i, ab, r in ((1, 0, 2), (3, 1, 1), (0, 0, 0), (2, 1, 0)):
+                arrived(x0.at[h, i], xrecv.at[0, h, i])
+                add_first(h, ab, r, x0.at[h, i])
+            begin(first_y(h))
+
+    def ev_first_y():
+        for h in range(NC):
+            for i in range(2):
+                arrived(y0.at[h, i], yrecv.at[0, h, i])
+                fbuf[0, i, :, cols(h)] = qbuf[0, h, i, 0, j].astype(f32) + y0[h, i].astype(f32)
+        ship(0)
+
+    def both(ev, n):
+        for h in range(NC):
+            ev(n, h)
 
     def m_copy(i):
         if i == 0:
@@ -702,22 +758,25 @@
             for base in (8, 12):
                 sm[s, base + r:base + r + 1, :] += smr[i, base + (r ^ flip):base + (r ^ flip) + 1, :]
 
+    def start_layer(l):
+        finish(u_copies(l, 1))
+        norm_bwd(dyv, u.at[1], inv.at[1], spv[l, 0, 6:7, :], dx, low, sm.at[l], 3, M)
+        xt[...] = low[...].T
+
     finish(first)
     sm[...] = jnp.zeros_like(sm)
+    start_layer(1)
+    begin(u_copies(0, 1))
+    pl.semaphore_wait(barrier, 3 + len(zn))
+    for src, dst, i in ((y_in, lo_out, 0), (rms_in, rm_out, 1)):
+        out_send(src, dst, i).start()
+        out_keep(src, dst, i).start()
 
     def layer(li, _):
         l = 1 - li
         n0 = 3 * li
         spl = spv.at[l, 0]
         sml = sm.at[l]
-        finish(u_copies(l, 1))
-        norm_bwd(dyv, u.at[1], inv.at[1], spl[6:7, :], dx, low, sml, 3, M)
-
-        @pl.when(li == 0)
-        def _():
-            begin(u_copies(0, 1))
-        xt[...] = low[...].T
-
         def down_step(ri, r):
             m = 4 * li + ri
             finish(g_copies(m))
@@ -728,9 +787,15 @@
                 begin(g_copies(m + 2))
         slots(n0, down_step)
 
+        @pl.when(li == 0)
+        def _():
+            if zin:
+                for h in range(NC):
+                    begin(first_z(h))
+
         @pl.when(li == 1)
         def _():
-            ev_y(1)
+            both(ev_y, 1)
         finish(u_copies(l, 0))
         low2[...] = (u[0] * spl[3:4, :] + spl[4:5, :]).astype(bf16)
         xt[...] = low2[...].T
@@ -745,12 +810,17 @@
             @pl.when(m + 2 < 8)
             def _():
                 begin(f_copies(m + 2))
+
+            @pl.when((li == 1) & (ri == 1))
+            def _():
+                both(ev_x, 2)
         slots(n0 + 1, up_step)
 
-        @pl.when(li == 1)
-        def _():
-            ev_x(2)
-            ev_z(0)
+        @pl.when(li == 0)
+        def _():
+            if not zin:
+                both(ev_x, 0)
+
         norm_bwd(dx, u.at[0], inv.at[0], spl[3:4, :], dx, low, sml, 0, M)
 
         @pl.when(li == 0)
@@ -777,16 +847,32 @@
 
             @pl.when((li == 0) & (ri == 1))
             def _():
-                ev_x(0)
-
-            @pl.when((li == 0) & (ri == 3))
-            def _():
-                ev_x(1)
-                ev_y(0)
+                both(ev_x, 1)
+
+            if not zin:
+                @pl.when((li == 0) & (ri == 2))
+                def _():
+                    both(ev_y, 0)
+
+            @pl.when((li == 1) & (ri == 0))
+            def _():
+                both(ev_x, 3)
+
+            @pl.when((li == 1) & (ri == 1))
+            def _():
+                both(ev_y, 2)
+                if zin:
+                    ev_first_z()
+
+            @pl.when((li == 1) & (ri == 2))
+            def _():
+                both(ev_x, 4)
 
             @pl.when((li == 1) & (ri == 3))
             def _():
-                ev_x(3)
+                both(ev_y, 3)
+                if zin:
+                    ev_first_x()
         slots(n0 + 2, attn_step)
         dyv[...] = dx[...].astype(bf16)
         own = l == s
@@ -806,6 +892,10 @@
         @pl.when(jnp.logical_not(own) & (li == 0))
         def _():
             dh_send().wait_send()
+
+        @pl.when(li == 0)
+        def _():
+            start_layer(0)
         return 0
 
     def dh_keep():
@@ -817,24 +907,23 @@
     lax.fori_loop(0, 2, layer, 0)
 
     m_copy(0).start()
-    ev_y(2)
+    both(ev_y, 4)
     m_add(0, 0)
     m_copy(1).start()
-    ev_z(1)
-    ev_x(4)
+    both(ev_x, 5)
+    if zin:
+        ev_first_y()
+    both(ev_z, 1)
+    both(ev_z, 2)
     m_add(1, 1)
     m_copy(2).start()
-    ev_y(3)
-    ev_z(2)
+    both(ev_y, 5)
+    both(ev_z, 3)
     m_add(2, 2)
     if zin:
         for d in range(1, n_dp):
             m_z(d).start()
-    ev_x(5)
-    ev_y(4)
-    ev_z(3)
-    ev_y(5)
-    ev_z(4)
+    both(ev_z, 4)
     if zin:
         for d in range(1, n_dp):
             m_z(d).wait_send()
@@ -842,20 +931,25 @@
             m_add(2 + d, 0)
     smc = pltpu.make_async_copy(sm.at[s], sm_out, ld.at[5])
     smc.start()
-    ev_z(5)
+    both(ev_z, 5)
 
     smc.wait()
     m_copy(0).wait_send()
     for r in range(4):
         d_copy(r).wait_send()
     for n in range(6):
-        for d in x_copies(n) + y_copies(n):
-            d.wait_send()
-        if zin:
-            for d in z_copies(n):
+        for h in range(NC):
+            if zin and n == 0:
+                for d in first_z(h) + [first_x(h, i) for i in range(4)] + first_y(h):
+                    d.wait_send()
+                continue
+            for d in [x_copy_of(n, h, i) for i in range(4)] + y_copies(n, h):
                 d.wait_send()
-        else:
-            q_copy(n).wait()
+            if zin:
+                for d in z_copies(n, h):
+                    d.wait_send()
+            else:
+                q_copy(n, h).wait()
     for src, dst, i in ((y_in, lo_out, 0), (rms_in, rm_out, 1)):
         out_send(src, dst, i).wait()
         out_keep(src, dst, i).wait()
@@ -880,14 +974,15 @@
     S = jax.ShapeDtypeStruct
     V = pltpu.VMEM
     any_ = pl.BlockSpec(memory_space=pl.ANY)
-    outs = (S((3, 2, 2, sub, 768), f32) if zin else S((2, 3, 2, NJ, sub, 768), bf16), S((16, 768), f32), S((2, M, D), bf16), S((2, M, D), bf16), S((2, 16, 128), f32))
+    outs = (S((3, 2, 2, sub, 768), f32) if zin else S((2, 3, NC, 2, NJ, sub, CW), bf16), S((16, 768), f32), S((2, M, D), bf16), S((2, M, D), bf16), S((2, 16, 128), f32))
     DMA = pltpu.SemaphoreType.DMA
     REG = pltpu.SemaphoreType.REGULAR
     bufs = [V((2, D, 768), bf16), V((2, D, 768), bf16), V((2, D, 768), bf16), V((2, M, FB), f32), V((2, M, FB), bf16), V((2, M, 3 * HB), bf16), V((2, nch, HPB, L, L), bf16), V((2, M, HB), bf16),
             V((2, M, D), f32), V((2, M, 1), f32), V((M, D), bf16), V((M, D), bf16), V((2, 4, 8, D), f32), V((M, D), f32), V((M, D), bf16), V((M, D), bf16), V((M, HB), bf16), V((M, 3 * HB), bf16), V((D, M), bf16), V((D, M), bf16),
-            V((4, 2, 2, NJ, sub, 768), bf16), V((4, 2, NJ, sub, 768), bf16), V((6, 2, 4, NJ, sub, 768), bf16), V((3, 4, NJ, sub, 768), bf16), V((6, 2, NJ, sub, 768), bf16),
-            V((6, 3, 2, sub, 768) if zin else (8, 128), bf16), V((6, 2, sub, 768) if zin else (8, 128), f32), V((2, 16, 768), f32), V((6, 16, 768), f32)]
-    sems = [DMA((2,)), DMA((2, 3)), DMA((2, 4)), DMA((7,)), DMA((4,)), DMA((4,)), DMA((6, 4)), DMA((6, 4)), DMA((6, 2)), DMA((6, 2)), DMA((6, 3)), DMA((6, 3)), DMA((3,)), DMA((3,)), DMA((6,)), DMA((6,)), DMA((6,)),
+            V((4, 2, 2, NJ, sub, 768), bf16), V((4, 2, NJ, sub, 768), bf16), V((6, NC, 2, 4, NJ, sub, CW), bf16), V((3, NC, 4, NJ, sub, CW), bf16), V((6, NC, 2, NJ, sub, CW), bf16),
+            V((6, NC, 3, 2, sub, CW) if zin else (8, 128), bf16), V((6, 2, sub, 768) if zin else (8, 128), f32), V((2, 16, 768), f32), V((6, 16, 768), f32),
+            V((NC, 3, 2, 4, sub, CW) if zin else (8, 128), bf16), V((NC, 4, sub, CW), bf16), V((NC, 2, sub, CW), bf16), pltpu.SemaphoreType.DMA((NC, 3)), pltpu.SemaphoreType.DMA((NC, 3))]
+    sems = [DMA((2,)), DMA((2, 3)), DMA((2, 4)), DMA((7,)), DMA((4,)), DMA((4,)), DMA((6, NC, 4)), DMA((6, NC, 4)), DMA((6, NC, 2)), DMA((6, NC, 2)), DMA((6, NC, 3)), DMA((6, NC, 3)), DMA((3,)), DMA((3,)), DMA((6, NC)), DMA((6,)), DMA((6,)),
             DMA((3,)), DMA((3,)), DMA((3,)), REG, REG, REG]
     return pl.pallas_call(
         functools.partial(k2_kernel, nch, L, n_dp, zin),
@@ -973,7 +1068,7 @@
         mine = grads[s].astype(f32)
         got = lax.ppermute(grads[1 - s], "section", [(0, 1), (1, 0)]).astype(f32)
         both = jnp.stack([jnp.where(s == 0, mine, got), jnp.where(s == 0, got, mine)])
-        both = both.transpose(1, 3, 0, 2, 4, 5).reshape(3, D, 768)
+        both = both.transpose(1, 4, 0, 3, 5, 2, 6).reshape(3, D, 768)
         grads = lax.psum_scatter(both, "dp", scatter_dimension=1, tiled=True)
         sm = lax.psum(sm, "dp")
     lo, dh, gu, gd, gq, qb, go, ub, vec, sums = run_finish(n_dp, nch, M, lengths, grads, sm, rm, lo, dh)

time: 273 us -> 256 us (0.938)
  Pallas kernels: 271 us -> 255 us
    pallas_call x1, Pallas kernels: 158 us -> 144 us  [run_k2(): pl.pallas_call(functools.partial(k2_kernel, nch, L, n_dp, zin), out_shape...]
where the time goes in v1:
time: 256 us
  Pallas kernels  255 us (100%)
    pallas_call x1, Pallas kernels, run_k2(): pl.pallas_call(functools.partial(k2_kernel, nch, L, n_dp, zin), out_shape...  144 us
    pallas_call x1, Pallas kernels, run_k1(): pl.pallas_call(functools.partial(k1_kernel, nch, L), out_shape=outs, in_s...  106 us
    pallas_call x1, Pallas kernels, run_finish(): pl.pallas_call(functools.partial(finish_kernel, n_dp, nch), out_shape=(S(...  6.01 us

profile of v1, /device:TPU:0, one launch (start us, length us, event | category | flops | bytes accessed | tf_op | source)
XLA Modules:
  0.0 256.3 jit_solution(11204536155164625279)
XLA Ops:
  0.6 105.8 %gather_forward.1 = (bf16[2,3,4,768,768]{4,3,2,1,0:T(8,128)(2,1)}, f32[2,4,8,768]{3,2,1,0:T(8,128)}, bf16[2,4,480,576]{3,2,1,0:T(8,128)(2,1)}, bf16[2,4,3,3,160,...) custom-call(s32[24]{0:T(128)} %len_ref.3, ...), custom_call_target="tpu_custom_call" | custom-call | tf_op jit(solution)/shard_map/gather_forward/pallas_call | solution.py:462
  106.5 143.6 %backward_reduce.1 = (f32[3,2,2,48,768]{4,3,2,1,0:T(8,128)}, f32[16,768]{1,0:T(8,128)}, bf16[2,480,768]{2,1,0:T(8,128)(2,1)}, bf16[2,480,768]{2,1,0:T(8,128)(2,1)}, f32[2,16,128]{2,1,0:T(8,128)}) custom-call(bf16[2,3,4,768,768]{4,3,2,1,0:T(8,128)(2,1)} %get-tuple-element.36.w_in, f32[2,4,8,768]{3,2,1,0:T(8,128)} %get-tuple-element.37.sp_in, ...), custom_call_target="tpu_custom_call" | custom-call | tf_op jit(solution)/shard_map/backward_reduce/pallas_call | solution.py:987
  250.1 6.0 %finish.1 = (bf16[2,480,768]{2,1,0:T(8,128)(2,1)}, bf16[2,480,768]{2,1,0:T(8,128)(2,1)}, f32[192,768]{1,0:T(8,128)}, f32[192,768]{1,0:T(8,128)}, f32[3,192,192]{...) custom-call(s32[24]{0:T(128)} %len_ref.3, ...), custom_call_target="tpu_custom_call" | custom-call | tf_op jit(solution)/shard_map/finish/pallas_call | solution.py:1042

commit v2 on v1

--- a/solution.py
+++ b/solution.py
@@ -474,6 +474,7 @@
 
 NJ = 4
 NC = 2
+ZF, HZ = 1, 1
 CW = 768 // NC
 
 
@@ -492,6 +493,7 @@
     xn = {"tensor": t + 1 - 2 * lax.rem(t, 2)}
     yn = {"tensor": t + 2 - 4 * lax.rem(t // 2, 2)}
     sib = {"section": 1 - s}
+    diag = {"tensor": 3 - t}
     zn = [{"dp": lax.rem(j + d, n_dp)} for d in range(1, n_dp)] if zin else []
 
     def remote(src, dst, ss, rs, dev):
@@ -538,17 +540,17 @@
     first = [pltpu.make_async_copy(dy_in.at[s], dyv, ld.at[5]), pltpu.make_async_copy(sp_in, spv, ld.at[6])]
     begin(first)
     begin(u_copies(1, 1))
-    begin(g_copies(0))
     begin(u_copies(1, 0))
-    begin(g_copies(1))
     begin(f_copies(0))
     begin(f_copies(1))
+    begin(g_copies(0))
+    begin(g_copies(1))
     begin(x_copy(y_in.at[0]))
     begin(a_copies(0))
     begin(a_copies(1))
 
     barrier = pltpu.get_barrier_semaphore()
-    for dev in [xn, yn, sib] + zn:
+    for dev in [xn, yn, diag, sib] + zn:
         pl.semaphore_signal(barrier, inc=1, device_id=dev, device_id_type=MESH)
 
     def out_send(src, dst, i):
@@ -597,27 +599,38 @@
         x_sends(n, r)
 
     def x_sends(n, r):
-        go = n >= (1 if zin else 0)
+        if zin:
+            go = (n < 5) | (r < 3)
+        else:
+            go = n >= 0
+        send_x(n, r, go)
+
+    def send_x(n, r, go):
+        def begin_x(*which):
+            for h in range(NC):
+                def start_them():
+                    for i in which:
+                        x_copy_of(n, h, i).start()
+                if zin and h < HZ:
+                    pl.when(n != ZF)(start_them)
+                else:
+                    start_them()
 
         @pl.when(go & (r == 3))
         def _():
-            @pl.when(n >= (4 if zin else 3))
+            @pl.when(n >= 3)
             def _():
                 pl.semaphore_wait(xcred, 1)
                 pl.semaphore_wait(ycred, 1)
-            for h in range(NC):
-                x_copy_of(n, h, 1).start()
-                x_copy_of(n, h, 3).start()
+            begin_x(1, 3)
 
         @pl.when(go & (r == 2))
         def _():
-            for h in range(NC):
-                x_copy_of(n, h, 2).start()
+            begin_x(2)
 
         @pl.when(go & (r == 1))
         def _():
-            for h in range(NC):
-                x_copy_of(n, h, 0).start()
+            begin_x(0)
 
     def slots(n, step):
         def body(ri, _):
@@ -646,7 +659,7 @@
             if i in (1, 3):
                 cs[i // 2].start()
         if h == NC - 1:
-            @pl.when((n < 3) & (n > 0) if zin else n < 3)
+            @pl.when(n < 3)
             def _():
                 pl.semaphore_signal(xcred, inc=1, device_id=xn, device_id_type=MESH)
                 pl.semaphore_signal(ycred, inc=1, device_id=yn, device_id_type=MESH)
@@ -656,7 +669,7 @@
 
     def q_copy(n, h):
         li = n // 3
-        return pltpu.make_async_copy(qbuf.at[n, h, :, 0], f_out.at[1 - li, 2 - (n - 3 * li), h], fl.at[n, h])
+        return pltpu.make_async_copy(qbuf.at[n, h, :, 0], f_out.at[1 - li, lax.rem(n + 1, 3), h], fl.at[n, h])
 
     def ev_y(n, h):
         for i in range(2):
@@ -668,10 +681,10 @@
             q_copy(n, h).start()
 
     def f_keep(n):
-        return pltpu.make_async_copy(fbuf.at[n], f_out.at[2 - lax.rem(n, 3), s], fl.at[lax.rem(n, 3), 0])
+        return pltpu.make_async_copy(fbuf.at[n], f_out.at[lax.rem(n + 1, 3), s], fl.at[lax.rem(n, 3), 0])
 
     def f_send(n):
-        return remote(fbuf.at[n], f_out.at[2 - lax.rem(n, 3), s], fsend.at[lax.rem(n, 3)], frecv.at[lax.rem(n, 3)], sib)
+        return remote(fbuf.at[n], f_out.at[lax.rem(n + 1, 3), s], fsend.at[lax.rem(n, 3)], frecv.at[lax.rem(n, 3)], sib)
 
     def ship(n):
         mine = (1 - n // 3) == s
@@ -697,45 +710,44 @@
         ship(n)
 
     def first_z(h):
-        return [remote(qbuf.at[0, h, :, :, lax.rem(j + d, n_dp)], z0.at[h, d - 1], z0send.at[h, d - 1], z0recv.at[h, d - 1], zn[d - 1]) for d in range(1, n_dp)]
+        return [remote(qbuf.at[ZF, h, :, :, lax.rem(j + d, n_dp)], z0.at[h, d - 1], z0send.at[h, d - 1], z0recv.at[h, d - 1], zn[d - 1]) for d in range(1, n_dp)]
 
     def first_x(h, i):
         ab, r, dev = ((0, 1, xn), (0, 3, xn), (1, 2, yn), (1, 3, yn))[i]
-        return remote(qbuf.at[0, h, ab, r, j], x0.at[h, i], xsend.at[0, h, i], xrecv.at[0, h, i], dev)
+        return remote(qbuf.at[ZF, h, ab, r, j], x0.at[h, i], xsend.at[ZF, h, i], xrecv.at[ZF, h, i], dev)
 
     def first_y(h):
-        return [remote(qbuf.at[0, h, 0, 2, j], y0.at[h, 0], ysend.at[0, h, 0], yrecv.at[0, h, 0], yn),
-                remote(qbuf.at[0, h, 1, 1, j], y0.at[h, 1], ysend.at[0, h, 1], yrecv.at[0, h, 1], xn)]
+        return [remote(qbuf.at[ZF, h, 0, 2, j], y0.at[h, 0], ysend.at[ZF, h, 0], yrecv.at[ZF, h, 0], yn),
+                remote(qbuf.at[ZF, h, 1, 1, j], y0.at[h, 1], ysend.at[ZF, h, 1], yrecv.at[ZF, h, 1], xn)]
 
     def add_first(h, ab, r, ref):
-        qbuf[0, h, ab, r, j] = (qbuf[0, h, ab, r, j].astype(f32) + ref[...].astype(f32)).astype(bf16)
+        qbuf[ZF, h, ab, r, j] = (qbuf[ZF, h, ab, r, j].astype(f32) + ref[...].astype(f32)).astype(bf16)
 
     def ev_first_z():
-        for h in range(NC):
+        for h in range(HZ):
             for d in range(n_dp - 1):
                 arrived(z0.at[h, d], z0recv.at[h, d])
             for ab in range(2):
                 for r in range(4):
-                    tot = qbuf[0, h, ab, r, j].astype(f32)
+                    tot = qbuf[ZF, h, ab, r, j].astype(f32)
                     for d in range(n_dp - 1):
                         tot = tot + z0[h, d, ab, r].astype(f32)
-                    qbuf[0, h, ab, r, j] = tot.astype(bf16)
+                    qbuf[ZF, h, ab, r, j] = tot.astype(bf16)
             for i in range(4):
                 first_x(h, i).start()
 
     def ev_first_x():
-        for h in range(NC):
+        for h in range(HZ):
             for i, ab, r in ((1, 0, 2), (3, 1, 1), (0, 0, 0), (2, 1, 0)):
-                arrived(x0.at[h, i], xrecv.at[0, h, i])
+                arrived(x0.at[h, i], xrecv.at[ZF, h, i])
                 add_first(h, ab, r, x0.at[h, i])
             begin(first_y(h))
 
     def ev_first_y():
-        for h in range(NC):
+        for h in range(HZ):
             for i in range(2):
-                arrived(y0.at[h, i], yrecv.at[0, h, i])
-                fbuf[0, i, :, cols(h)] = qbuf[0, h, i, 0, j].astype(f32) + y0[h, i].astype(f32)
-        ship(0)
+                arrived(y0.at[h, i], yrecv.at[ZF, h, i])
+                fbuf[ZF, i, :, cols(h)] = qbuf[ZF, h, i, 0, j].astype(f32) + y0[h, i].astype(f32)
 
     def both(ev, n):
         for h in range(NC):
@@ -744,30 +756,32 @@
     def m_copy(i):
         if i == 0:
             return remote(sm.at[1 - s], smr.at[0], msend.at[0], mrecv.at[0], sib)
-        return remote(sm.at[s], smr.at[i], msend.at[i], mrecv.at[i], xn if i == 1 else yn)
+        return remote(sm.at[s], smr.at[i], msend.at[i], mrecv.at[i], (xn, yn, diag)[i - 1])
 
     def m_z(d):
-        return remote(sm.at[s], smr.at[2 + d], msend.at[2 + d], mrecv.at[2 + d], zn[d - 1])
+        return remote(sm.at[s], smr.at[3 + d], msend.at[3 + d], mrecv.at[3 + d], zn[d - 1])
 
     def m_add(i, flip):
         arrived(smr.at[i], mrecv.at[i])
-        if i in (1, 2):
-            m_copy(i).wait_send()
         sm[s, 0:8, :] += smr[i, 0:8, :]
         for r in range(4):
             for base in (8, 12):
                 sm[s, base + r:base + r + 1, :] += smr[i, base + (r ^ flip):base + (r ^ flip) + 1, :]
 
+    def rest(ev, n):
+        for h in range(HZ if zin else 0, NC):
+            ev(n, h)
+
     def start_layer(l):
         finish(u_copies(l, 1))
         norm_bwd(dyv, u.at[1], inv.at[1], spv[l, 0, 6:7, :], dx, low, sm.at[l], 3, M)
-        xt[...] = low[...].T
+        xt2[...] = low[...].T
 
     finish(first)
     sm[...] = jnp.zeros_like(sm)
     start_layer(1)
     begin(u_copies(0, 1))
-    pl.semaphore_wait(barrier, 3 + len(zn))
+    pl.semaphore_wait(barrier, 4 + len(zn))
     for src, dst, i in ((y_in, lo_out, 0), (rms_in, rm_out, 1)):
         out_send(src, dst, i).start()
         out_keep(src, dst, i).start()
@@ -777,25 +791,6 @@
         n0 = 3 * li
         spl = spv.at[l, 0]
         sml = sm.at[l]
-        def down_step(ri, r):
-            m = 4 * li + ri
-            finish(g_copies(m))
-            put(n0, r, dot(xt[...], g[lax.rem(m, 2)]))
-
-            @pl.when(m + 2 < 8)
-            def _():
-                begin(g_copies(m + 2))
-        slots(n0, down_step)
-
-        @pl.when(li == 0)
-        def _():
-            if zin:
-                for h in range(NC):
-                    begin(first_z(h))
-
-        @pl.when(li == 1)
-        def _():
-            both(ev_y, 1)
         finish(u_copies(l, 0))
         low2[...] = (u[0] * spl[3:4, :] + spl[4:5, :]).astype(bf16)
         xt[...] = low2[...].T
@@ -805,22 +800,37 @@
             b = lax.rem(m, 2)
             finish(f_copies(m))
             ffn_bwd_block(low, wu.at[b], wd.at[b], gp.at[b], low2, dx, sml.at[pl.ds(8 + r, 1)])
-            put(n0 + 1, r, dot(xt[...], low2[...]))
+            put(n0, r, dot(xt[...], low2[...]))
 
             @pl.when(m + 2 < 8)
             def _():
                 begin(f_copies(m + 2))
-
-            @pl.when((li == 1) & (ri == 1))
-            def _():
-                both(ev_x, 2)
-        slots(n0 + 1, up_step)
-
-        @pl.when(li == 0)
-        def _():
-            if not zin:
-                both(ev_x, 0)
-
+        slots(n0, up_step)
+
+        @pl.when(li == 1)
+        def _():
+            both(ev_x, 2)
+
+        def down_step(ri, r):
+            m = 4 * li + ri
+            finish(g_copies(m))
+            put(n0 + 1, r, dot(xt2[...], g[lax.rem(m, 2)]))
+
+            @pl.when(m + 2 < 8)
+            def _():
+                begin(g_copies(m + 2))
+        slots(n0 + 1, down_step)
+
+        if zin:
+            @pl.when(li == 1)
+            def _():
+                ev_first_z()
+
+        if zin:
+            @pl.when(li == 0)
+            def _():
+                for h in range(HZ):
+                    begin(first_z(h))
         norm_bwd(dx, u.at[0], inv.at[0], spl[3:4, :], dx, low, sml, 0, M)
 
         @pl.when(li == 0)
@@ -845,14 +855,21 @@
             def _():
                 begin(a_copies(m + 2))
 
+            @pl.when((li == 0) & (ri == 0))
+            def _():
+                both(ev_x, 0)
+
             @pl.when((li == 0) & (ri == 1))
             def _():
-                both(ev_x, 1)
-
-            if not zin:
-                @pl.when((li == 0) & (ri == 2))
-                def _():
-                    both(ev_y, 0)
+                rest(ev_x, 1)
+
+            @pl.when((li == 0) & (ri == 2))
+            def _():
+                both(ev_y, 0)
+
+            @pl.when((li == 0) & (ri == 3))
+            def _():
+                rest(ev_y, 1)
 
             @pl.when((li == 1) & (ri == 0))
             def _():
@@ -861,12 +878,12 @@
             @pl.when((li == 1) & (ri == 1))
             def _():
                 both(ev_y, 2)
+
+            @pl.when((li == 1) & (ri == 2))
+            def _():
+                both(ev_x, 4)
                 if zin:
-                    ev_first_z()
-
-            @pl.when((li == 1) & (ri == 2))
-            def _():
-                both(ev_x, 4)
+                    send_x(5, 3, True)
 
             @pl.when((li == 1) & (ri == 3))
             def _():
@@ -909,26 +926,29 @@
     m_copy(0).start()
     both(ev_y, 4)
     m_add(0, 0)
-    m_copy(1).start()
+    for i in (1, 2, 3):
+        m_copy(i).start()
     both(ev_x, 5)
     if zin:
         ev_first_y()
-    both(ev_z, 1)
+    both(ev_z, 0)
+    rest(ev_z, 1)
     both(ev_z, 2)
-    m_add(1, 1)
-    m_copy(2).start()
-    both(ev_y, 5)
-    both(ev_z, 3)
-    m_add(2, 2)
+    for i in (1, 2, 3):
+        m_copy(i).wait_send()
+    for i in (1, 2, 3):
+        m_add(i, i)
     if zin:
         for d in range(1, n_dp):
             m_z(d).start()
+    both(ev_y, 5)
+    both(ev_z, 3)
     both(ev_z, 4)
     if zin:
         for d in range(1, n_dp):
             m_z(d).wait_send()
         for d in range(1, n_dp):
-            m_add(2 + d, 0)
+            m_add(3 + d, 0)
     smc = pltpu.make_async_copy(sm.at[s], sm_out, ld.at[5])
     smc.start()
     both(ev_z, 5)
@@ -939,7 +959,7 @@
         d_copy(r).wait_send()
     for n in range(6):
         for h in range(NC):
-            if zin and n == 0:
+            if zin and n == ZF and h < HZ:
                 for d in first_z(h) + [first_x(h, i) for i in range(4)] + first_y(h):
                     d.wait_send()
                 continue
@@ -962,7 +982,7 @@
     arrived(dh_out.at[1 - s], orecv.at[2])
     if zin:
         for k in range(3):
-            arrived(f_out.at[2 - k, 1 - s], frecv.at[k])
+            arrived(f_out.at[(k + 1) % 3, 1 - s], frecv.at[k])
             f_keep(k).wait()
             f_send(k).wait_send()
 
@@ -980,9 +1000,9 @@
     bufs = [V((2, D, 768), bf16), V((2, D, 768), bf16), V((2, D, 768), bf16), V((2, M, FB), f32), V((2, M, FB), bf16), V((2, M, 3 * HB), bf16), V((2, nch, HPB, L, L), bf16), V((2, M, HB), bf16),
             V((2, M, D), f32), V((2, M, 1), f32), V((M, D), bf16), V((M, D), bf16), V((2, 4, 8, D), f32), V((M, D), f32), V((M, D), bf16), V((M, D), bf16), V((M, HB), bf16), V((M, 3 * HB), bf16), V((D, M), bf16), V((D, M), bf16),
             V((4, 2, 2, NJ, sub, 768), bf16), V((4, 2, NJ, sub, 768), bf16), V((6, NC, 2, 4, NJ, sub, CW), bf16), V((3, NC, 4, NJ, sub, CW), bf16), V((6, NC, 2, NJ, sub, CW), bf16),
-            V((6, NC, 3, 2, sub, CW) if zin else (8, 128), bf16), V((6, 2, sub, 768) if zin else (8, 128), f32), V((2, 16, 768), f32), V((6, 16, 768), f32),
-            V((NC, 3, 2, 4, sub, CW) if zin else (8, 128), bf16), V((NC, 4, sub, CW), bf16), V((NC, 2, sub, CW), bf16), pltpu.SemaphoreType.DMA((NC, 3)), pltpu.SemaphoreType.DMA((NC, 3))]
-    sems = [DMA((2,)), DMA((2, 3)), DMA((2, 4)), DMA((7,)), DMA((4,)), DMA((4,)), DMA((6, NC, 4)), DMA((6, NC, 4)), DMA((6, NC, 2)), DMA((6, NC, 2)), DMA((6, NC, 3)), DMA((6, NC, 3)), DMA((3,)), DMA((3,)), DMA((6, NC)), DMA((6,)), DMA((6,)),
+            V((6, NC, 3, 2, sub, CW) if zin else (8, 128), bf16), V((6, 2, sub, 768) if zin else (8, 128), f32), V((2, 16, 768), f32), V((7, 16, 768), f32),
+            V((HZ, 3, 2, 4, sub, CW) if zin else (8, 128), bf16), V((NC, 4, sub, CW), bf16), V((NC, 2, sub, CW), bf16), pltpu.SemaphoreType.DMA((NC, 3)), pltpu.SemaphoreType.DMA((NC, 3))]
+    sems = [DMA((2,)), DMA((2, 3)), DMA((2, 4)), DMA((7,)), DMA((4,)), DMA((4,)), DMA((6, NC, 4)), DMA((6, NC, 4)), DMA((6, NC, 2)), DMA((6, NC, 2)), DMA((6, NC, 3)), DMA((6, NC, 3)), DMA((3,)), DMA((3,)), DMA((6, NC)), DMA((7,)), DMA((7,)),
             DMA((3,)), DMA((3,)), DMA((3,)), REG, REG, REG]
     return pl.pallas_call(
         functools.partial(k2_kernel, nch, L, n_dp, zin),

time: 256 us -> 251 us (0.980)
  Pallas kernels: 255 us -> 250 us
    pallas_call x1, Pallas kernels: 144 us -> 138 us  [run_k2(): pl.pallas_call(functools.partial(k2_kernel, nch, L, n_dp, zin), out_shape...]
where the time goes in v2:
time: 251 us
  Pallas kernels  250 us (100%)
    pallas_call x1, Pallas kernels, run_k2(): pl.pallas_call(functools.partial(k2_kernel, nch, L, n_dp, zin), out_shape...  138 us
    pallas_call x1, Pallas kernels, run_k1(): pl.pallas_call(functools.partial(k1_kernel, nch, L), out_shape=outs, in_s...  106 us
    pallas_call x1, Pallas kernels, run_finish(): pl.pallas_call(functools.partial(finish_kernel, n_dp, nch), out_shape=(S(...  6.01 us

profile of v2, /device:TPU:0, one launch (start us, length us, event | category | flops | bytes accessed | tf_op | source)
XLA Modules:
  0.0 250.5 jit_solution(6256869280517476036)
XLA Ops:
  0.6 105.8 %gather_forward.1 = (bf16[2,3,4,768,768]{4,3,2,1,0:T(8,128)(2,1)}, f32[2,4,8,768]{3,2,1,0:T(8,128)}, bf16[2,4,480,576]{3,2,1,0:T(8,128)(2,1)}, bf16[2,4,3,3,160,...) custom-call(s32[24]{0:T(128)} %len_ref.3, ...), custom_call_target="tpu_custom_call" | custom-call | tf_op jit(solution)/shard_map/gather_forward/pallas_call | solution.py:462
  106.5 137.9 %backward_reduce.1 = (f32[3,2,2,48,768]{4,3,2,1,0:T(8,128)}, f32[16,768]{1,0:T(8,128)}, bf16[2,480,768]{2,1,0:T(8,128)(2,1)}, bf16[2,480,768]{2,1,0:T(8,128)(2,1)}, f32[2,16,128]{2,1,0:T(8,128)}) custom-call(bf16[2,3,4,768,768]{4,3,2,1,0:T(8,128)(2,1)} %get-tuple-element.36.w_in, f32[2,4,8,768]{3,2,1,0:T(8,128)} %get-tuple-element.37.sp_in, ...), custom_call_target="tpu_custom_call" | custom-call | tf_op jit(solution)/shard_map/backward_reduce/pallas_call | solution.py:1007
  244.3 6.0 %finish.1 = (bf16[2,480,768]{2,1,0:T(8,128)(2,1)}, bf16[2,480,768]{2,1,0:T(8,128)(2,1)}, f32[192,768]{1,0:T(8,128)}, f32[192,768]{1,0:T(8,128)}, f32[3,192,192]{...) custom-call(s32[24]{0:T(128)} %len_ref.3, ...), custom_call_target="tpu_custom_call" | custom-call | tf_op jit(solution)/shard_map/finish/pallas_call | solution.py:1062

commit v3 on v2

--- a/solution.py
+++ b/solution.py
@@ -1017,18 +1017,20 @@
 def finish_kernel(n_dp, nch, len_ref, f_in, sm_in, rm_in, lo_in, dh_in, lo_out, dh_out, gu, gd, gq, qb, go, ub, vec, sums, f_ref, sm_ref, rm_ref, lo_ref, dh_ref, sem):
     t = lax.axis_index("tensor")
     j = lax.axis_index("dp")
-    loads = [pltpu.make_async_copy(src, dst, sem.at[i]) for i, (src, dst) in enumerate(((f_in, f_ref), (sm_in, sm_ref), (rm_in, rm_ref), (lo_in, lo_ref), (dh_in, dh_ref)))]
-    stores = [pltpu.make_async_copy(src, dst, sem.at[5 + i]) for i, (src, dst) in enumerate(((f_ref.at[1], gu), (f_ref.at[2], gd), (lo_ref, lo_out), (dh_ref, dh_out)))]
+    loads = [pltpu.make_async_copy(src, dst, sem.at[i]) for i, (src, dst) in enumerate(((f_in.at[0], f_ref.at[0]), (sm_in, sm_ref), (rm_in, rm_ref), (lo_in, lo_ref), (dh_in, dh_ref), (f_in.at[1], f_ref.at[1]), (f_in.at[2], f_ref.at[2])))]
+    stores = [pltpu.make_async_copy(src, dst, sem.at[7 + i]) for i, (src, dst) in enumerate(((lo_ref, lo_out), (dh_ref, dh_out), (f_ref.at[1], gu), (f_ref.at[2], gd)))]
     for d in loads:
         d.start()
-    for d in loads:
-        d.wait()
-    for d in stores:
-        d.start()
+    loads[0].wait()
     ga = f_ref[0]
     for i in range(3):
         gq[i] = ga[:, i * HB:(i + 1) * HB]
     go[...] = ga[:, 3 * HB:4 * HB].T
+    for i in range(4):
+        loads[3 + i].wait()
+        stores[i].start()
+    loads[1].wait()
+    loads[2].wait()
     part = HS // n_dp
     share = D // (4 * n_dp)
     off = (j * 4 + t) * share
@@ -1065,7 +1067,7 @@
                    S((FB // HS, 1, part), f32), S((6, 1, D // (4 * n_dp)), f32), S((3, 1, 2 * nch), f32)),
         in_specs=[pl.BlockSpec(memory_space=pltpu.SMEM)] + [any_] * 5,
         out_specs=[any_] * 4 + [vm] * 6,
-        scratch_shapes=[V((3, dd, FB), f32), V((16, D), f32), V((2, 16, 128), f32), V((2, M, D), bf16), V((2, M, D), bf16), pltpu.SemaphoreType.DMA((9,))],
+        scratch_shapes=[V((3, dd, FB), f32), V((16, D), f32), V((2, 16, 128), f32), V((2, M, D), bf16), V((2, M, D), bf16), pltpu.SemaphoreType.DMA((11,))],
         compiler_params=pltpu.CompilerParams(vmem_limit_bytes=60 << 20),
         name="finish",
     )(lengths, f, sm, rm, lo, dh)

time: 251 us -> 250 us (level)
  no operation moved by 1% of the time
where the time goes in v3:
time: 250 us
  Pallas kernels  249 us (100%)
    pallas_call x1, Pallas kernels, run_k2(): pl.pallas_call(functools.partial(k2_kernel, nch, L, n_dp, zin), out_shape...  138 us
    pallas_call x1, Pallas kernels, run_k1(): pl.pallas_call(functools.partial(k1_kernel, nch, L), out_shape=outs, in_s...  106 us
    pallas_call x1, Pallas kernels, run_finish(): pl.pallas_call(functools.partial(finish_kernel, n_dp, nch), out_shape=(S(...  5.22 us

profile of v3, /device:TPU:0, one launch (start us, length us, event | category | flops | bytes accessed | tf_op | source)
XLA Modules:
  0.0 249.7 jit_solution(16918980274935163877)
XLA Ops:
  0.6 105.8 %gather_forward.1 = (bf16[2,3,4,768,768]{4,3,2,1,0:T(8,128)(2,1)}, f32[2,4,8,768]{3,2,1,0:T(8,128)}, bf16[2,4,480,576]{3,2,1,0:T(8,128)(2,1)}, bf16[2,4,3,3,160,...) custom-call(s32[24]{0:T(128)} %len_ref.3, ...), custom_call_target="tpu_custom_call" | custom-call | tf_op jit(solution)/shard_map/gather_forward/pallas_call | solution.py:462
  106.5 137.9 %backward_reduce.1 = (f32[3,2,2,48,768]{4,3,2,1,0:T(8,128)}, f32[16,768]{1,0:T(8,128)}, bf16[2,480,768]{2,1,0:T(8,128)(2,1)}, bf16[2,480,768]{2,1,0:T(8,128)(2,1)}, f32[2,16,128]{2,1,0:T(8,128)}) custom-call(bf16[2,3,4,768,768]{4,3,2,1,0:T(8,128)(2,1)} %get-tuple-element.36.w_in, f32[2,4,8,768]{3,2,1,0:T(8,128)} %get-tuple-element.37.sp_in, ...), custom_call_target="tpu_custom_call" | custom-call | tf_op jit(solution)/shard_map/backward_reduce/pallas_call | solution.py:1007
  244.3 5.2 %finish.1 = (bf16[2,480,768]{2,1,0:T(8,128)(2,1)}, bf16[2,480,768]{2,1,0:T(8,128)(2,1)}, f32[192,768]{1,0:T(8,128)}, f32[192,768]{1,0:T(8,128)}, f32[3,192,192]{...) custom-call(s32[24]{0:T(128)} %len_ref.3, ...), custom_call_target="tpu_custom_call" | custom-call | tf_op jit(solution)/shard_map/finish/pallas_call | solution.py:1064
